TPU v7x, 512 devices: a whole 4x4x16 slice. The times are simulated.
512 devices in a mesh: inst: 8 (over y, core), space: 64 (over x, z).
Axes of the slice: x: 4, y: 4, z: 16, core: 2. Of those that a mesh axis runs over, the one named last changes fastest.
Arguments:
- amplitudes: float32 [8, 40], replicated, may hold values from -6 to 6
- modal_coeffs: float32 [40, 3, 4096], P(None, None, ('inst', 'space')), may hold values from -0.6 to 0.6
- centre_positions: float32 [3, 4096], P(None, ('inst', 'space')), may hold values from 0 to 256
- base_nodes: float32 [3, 128, 64, 256], P(None, 'space'), may hold values from -1 to 256
Outputs:
- displacement: float32 [8, 3, 128, 64, 256], P('inst', None, 'space')
- metrics: float32 [8, 10, 128, 64, 256], P('inst', None, 'space')
All inputs are finite; a program needn't handle non-finite values.
Results may differ from a plain program's by a relative error of at most 0.0003.
Values sent between devices are 32-bit elements; how exact they have to be, the bound alone decides.
A program may use at most 64 MiB of HBM per device.

v0:
```python
import math

import jax
import jax.numpy as jnp
from jax import lax
from jax.sharding import PartitionSpec as P

support = 4.0


def padded_2(cells, sides, width):
    for axis, dim in sides:
        count = lax.axis_size(axis)
        ends = count - 1
        head = lax.slice_in_dim(cells, 0, width, axis=dim)
        tail = lax.slice_in_dim(cells, cells.shape[dim] - width, cells.shape[dim], axis=dim)
        cells = jnp.concatenate(
            [
                lax.ppermute(tail, axis, [(i, (i + 1) % count) for i in range(ends)]),
                cells,
                lax.ppermute(head, axis, [((i + 1) % count, i) for i in range(ends)]),
            ],
            axis=dim,
        )
    return cells


def kernel_tile(centres, node_list):
    separation = centres[0][:, None] - node_list[0][None, :]
    square = separation * separation
    separation = centres[1][:, None] - node_list[1][None, :]
    square = square + separation * separation
    separation = centres[2][:, None] - node_list[2][None, :]
    square = square + separation * separation
    radius = jnp.sqrt(square) / support
    inside = jnp.maximum(1.0 - radius, 0.0)
    inside_sq = inside * inside
    return inside_sq * inside_sq * (4.0 * radius + 1.0)


def accumulate(running, centre_moves, centres, node_list):
    length = centres.shape[1]
    block_size = math.gcd(length, 256)
    turns = length // block_size
    row_count = running.shape[0]
    node_total = node_list.shape[1]
    node_block = math.gcd(node_total, 2048)
    node_turns = node_total // node_block

    def over_centres(partial_value, nodes):

        def add_block(number, sofar):
            begin_at = jnp.asarray(number, jnp.int32) * block_size
            piece_moves = lax.dynamic_slice_in_dim(centre_moves, begin_at, block_size, 1)
            piece_centres = lax.dynamic_slice_in_dim(centres, begin_at, block_size, 1)
            tile = kernel_tile(piece_centres, nodes)
            return sofar + jnp.dot(
                piece_moves,
                tile,
                precision=lax.Precision.HIGHEST,
                preferred_element_type=jnp.float32,
            )

        return lax.fori_loop(0, turns, add_block, partial_value)

    stacked_nodes = node_list.reshape(3, node_turns, node_block).transpose(1, 0, 2)
    stacked_running = running.reshape(row_count, node_turns, node_block).transpose(1, 0, 2)

    def one_pair(paired):
        return over_centres(paired[0], paired[1])

    result = lax.map(one_pair, (stacked_running, stacked_nodes))
    return result.transpose(1, 0, 2).reshape(row_count, node_total)


def central(values, which_dim):
    extent = values.shape[which_dim]
    head_row = lax.slice_in_dim(values, 0, 1, axis=which_dim)
    second = lax.slice_in_dim(values, 1, 2, axis=which_dim)
    tail_row = lax.slice_in_dim(values, extent - 1, extent, axis=which_dim)
    before = lax.slice_in_dim(values, extent - 2, extent - 1, axis=which_dim)
    extended = jnp.concatenate(
        [2.0 * head_row - second, values, 2.0 * tail_row - before], axis=which_dim
    )
    upper_part = lax.slice_in_dim(extended, 2, extent + 2, axis=which_dim)
    lower_part = lax.slice_in_dim(extended, 0, extent, axis=which_dim)
    return (upper_part - lower_part) * 0.5


def cross_product(left_arm, right_arm):
    return jnp.stack(
        [
            left_arm[:, 1] * right_arm[:, 2] - left_arm[:, 2] * right_arm[:, 1],
            left_arm[:, 2] * right_arm[:, 0] - left_arm[:, 0] * right_arm[:, 2],
            left_arm[:, 0] * right_arm[:, 1] - left_arm[:, 1] * right_arm[:, 0],
        ],
        axis=1,
    )


def metric_stack(along_i, along_j, along_k):
    first_vec = cross_product(along_j, along_k)
    second_vec = cross_product(along_k, along_i)
    third_vec = cross_product(along_i, along_j)
    jacobian = (
        along_i[:, 0] * first_vec[:, 0]
        + along_i[:, 1] * first_vec[:, 1]
        + along_i[:, 2] * first_vec[:, 2]
    )
    return jnp.concatenate([first_vec, second_vec, third_vec, jacobian[:, None]], axis=1)


def body(amplitudes, modal_coeffs, centre_positions, base_nodes):
    count_inst = amplitudes.shape[0]
    local_centres = centre_positions.shape[1]
    groups = lax.axis_size("inst")
    own_count = count_inst // groups
    centre_moves = jnp.einsum(
        "tm,mcn->tcn", amplitudes, modal_coeffs, precision=lax.Precision.HIGHEST
    )
    node_list = base_nodes.reshape(3, -1)
    node_count = node_list.shape[1]
    share = node_count // groups
    my_nodes = lax.dynamic_slice_in_dim(node_list, lax.axis_index("inst") * share, share, 1)
    flat_moves = centre_moves.reshape(count_inst * 3, local_centres)
    start_value = jnp.zeros((count_inst * 3, share), jnp.float32)
    every_moves, every_centre = (
        lax.all_gather(flat_moves, ("inst", "space"), axis=1, tiled=True),
        lax.all_gather(centre_positions, ("inst", "space"), axis=1, tiled=True),
    )
    summed = accumulate(start_value, every_moves, every_centre, my_nodes)
    moved = lax.all_to_all(
        summed.reshape(count_inst, 3, share), "inst", split_axis=0, concat_axis=2, tiled=True
    )
    displacement = moved.reshape((own_count, 3) + base_nodes.shape[1:])
    deformed = base_nodes[None] + displacement
    padded = padded_2(deformed, (("space", 2),), 1)
    width = padded.shape[2]
    position = lax.axis_index("space")
    lower = jnp.where(position == 0, 2.0 * padded[:, :, 1:2] - padded[:, :, 2:3], padded[:, :, 0:1])
    upper = jnp.where(
        position == lax.axis_size("space") - 1,
        2.0 * padded[:, :, width - 2 : width - 1] - padded[:, :, width - 3 : width - 2],
        padded[:, :, width - 1 : width],
    )
    extended = jnp.concatenate([lower, padded[:, :, 1 : width - 1], upper], axis=2)
    along_i = (extended[:, :, 2:] - extended[:, :, :-2]) * 0.5
    along_j = central(deformed, 3)
    along_k = central(deformed, 4)
    return (displacement, metric_stack(along_i, along_j, along_k))


def solution(mesh):
    in_specs = (
        P(),
        P(None, None, ("inst", "space")),
        P(None, ("inst", "space")),
        P(None, "space", None, None),
    )
    out_specs = (P("inst", None, "space", None, None), P("inst", None, "space", None, None))
    return jax.shard_map(body, mesh=mesh, in_specs=in_specs, out_specs=out_specs, check_vma=False)
```

profile of v0, /device:TPU:1, one launch (start us, length us, event | category | flops | bytes accessed | tf_op | source)
XLA Modules:
  0.0 383.1 jit_solution(5147750935168183662)
XLA Ops:
  0.7 0.7 copy-done
  1.3 0.9 fusion.36
  2.4 1.3 copy.21
  3.6 138.7 %all-gather = f32[512,8,3]{1,2,0:T(4,128)S(1)} all-gather(f32[1,8,3]{1,2,0:T(4,128)} %bitcast.64), channel_id=1, replica_groups=mesh['inst'=8,'space'=64] {'inst','space'}, dimensions={0}, use_global_device_ids=true | all-gather | bytes 49248 | tf_op jit(solution)/shard_map/all_gather | solution.py:129
  142.4 0.4 reshape.152
  142.8 117.5 %all_gather.6 = f32[24,4096]{0,1:T(8,128)S(1)} all-gather(f32[24,8]{0,1:T(8,128)S(1)} %copy.15), channel_id=1, replica_groups=mesh['inst'=8,'space'=64] {'inst','space'}, dimensions={1}, use_global_device_ids=true | all-gather | bytes 393984 | tf_op jit(solution)/shard_map/all_gather | solution.py:128
  260.3 0.6 copy.17
  260.9 88.9 %while.36 = (s32[]{:T(128)}, f32[2,24,2048]{2,1,0:T(8,128)S(1)}, f32[2,3,2048]{2,1,0:T(4,128)S(1)}, f32[24,4096]{1,0:T(8,128)S(1)}, f32[3,4096]{1,0:T(4,128)S(1)...) while((s32[]{:T(128)}, f32[2,24,2048]{2,1,0:T(8,128)S(1)}, ...), condition=%wide.region_3.4_spmd, body=%wide.region_0.3_spmd.sunk | while | flops 158957568 | bytes 943554 | solution.py:72
  260.9 44.4 %while.37 = (s32[]{:T(128)}, f32[24,2048]{1,0:T(8,128)S(1)}, f32[24,4096]{1,0:T(8,128)S(1)}, f32[3,4096]{1,0:T(4,128)S(1)}, f32[3,2048]{1,0:T(4,128)S(1)}, /*ind...) while((s32[]{:T(128)}, f32[24,2048]{1,0:T(8,128)S(1)}, ...), condition=%wide.region_2.2_spmd.clone, body=%wide.region_1.1_spmd.clone.sunk | while | flops 158957568 | bytes 500949 | solution.py:64
  261.1 2.6 convolution_add_fusion.2
  263.8 2.6 convolution_add_fusion.2
  266.5 0.1 constant_dynamic-slice_fusion.3
  266.6 2.6 convolution_add_fusion.2
  269.3 0.1 constant_dynamic-slice_fusion.3
  269.4 2.6 convolution_add_fusion.2
  272.1 0.1 constant_dynamic-slice_fusion.3
  272.2 2.6 convolution_add_fusion.2
  274.9 2.6 convolution_add_fusion.2
  277.7 2.6 convolution_add_fusion.2
  280.4 0.1 constant_dynamic-slice_fusion.3
  280.5 2.6 convolution_add_fusion.2
  283.2 0.1 constant_dynamic-slice_fusion.3
  283.3 2.6 convolution_add_fusion.2
  285.9 0.1 constant_dynamic-slice_fusion.3
  286.0 2.6 convolution_add_fusion.2
  288.8 2.6 convolution_add_fusion.2
  291.6 2.6 convolution_add_fusion.2
  294.2 0.1 constant_dynamic-slice_fusion.3
  294.4 2.6 convolution_add_fusion.2
  297.0 0.1 constant_dynamic-slice_fusion.3
  297.1 2.6 convolution_add_fusion.2
  299.8 0.1 constant_dynamic-slice_fusion.3
  299.9 2.6 convolution_add_fusion.2
  302.7 2.6 convolution_add_fusion.2
  305.4 44.4 %while.37 = (s32[]{:T(128)}, f32[24,2048]{1,0:T(8,128)S(1)}, f32[24,4096]{1,0:T(8,128)S(1)}, f32[3,4096]{1,0:T(4,128)S(1)}, f32[3,2048]{1,0:T(4,128)S(1)}, /*ind...) while((s32[]{:T(128)}, f32[24,2048]{1,0:T(8,128)S(1)}, ...), condition=%wide.region_2.2_spmd.clone, body=%wide.region_1.1_spmd.clone.sunk | while | flops 158957568 | bytes 500949 | solution.py:64
  305.5 2.6 convolution_add_fusion.2
  308.3 2.6 convolution_add_fusion.2
  311.1 2.6 convolution_add_fusion.2
  313.8 2.6 convolution_add_fusion.2
  316.6 2.6 convolution_add_fusion.2
  319.4 2.6 convolution_add_fusion.2
  322.2 2.6 convolution_add_fusion.2
  324.9 2.6 convolution_add_fusion.2
  327.7 2.6 convolution_add_fusion.2
  330.5 2.6 convolution_add_fusion.2
  333.3 2.6 convolution_add_fusion.2
  336.0 2.6 convolution_add_fusion.2
  338.8 2.6 convolution_add_fusion.2
  341.6 2.6 convolution_add_fusion.2
  344.4 2.6 convolution_add_fusion.2
  347.1 2.6 convolution_add_fusion.2
  349.8 0.3 copy.18
  350.1 1.2 reshape_reshape.3
  351.4 10.6 %all-to-all-start = ((f32[8,3,4096]{2,1,0:T(4,128)}), f32[8,3,4096]{2,1,0:T(4,128)S(1)}, u32[]{:S(2)}, u32[]{:S(2)}) async-start(f32[8,3,4096]{2,1,0:T(4,128)} %reshape_reshape.3), calls=%async_computation | async-start | bytes 1048576 | tf_op jit(solution)/shard_map/all_to_all | solution.py:132
  361.9 9.5 %all-to-all-done = f32[8,3,4096]{2,1,0:T(4,128)S(1)} async-done(((f32[8,3,4096]{2,1,0:T(4,128)}), f32[8,3,4096]{2,1,0:T(4,128)S(1)}, u32[]{:S(2)}, u32[]{:S(2)}) %all-to-all-start) | async-done | bytes 393248 | tf_op jit(solution)/shard_map/all_to_all | solution.py:132
  371.4 0.2 copy.19
  371.7 0.8 reshape.149
  372.6 0.2 slice_subtract_fusion.1
  372.9 1.3 collective-permute-start
  374.2 4.0 %collective-permute-start.1 = (f32[1,3,1,64,256]{4,3,2,1,0:T(8,128)S(1)}, f32[1,3,1,64,256]{4,3,2,1,0:T(8,128)S(1)}, u32[]{:S(2)}, u32[]{:S(2)}) collective-permute-start(f32[1,3,1,64,256]{4,3,2,1,0:T(8,128)S(1)} %get-tuple-element.277), channel_id=1, source_target_pairs={{0,1},{1,2},{2,3},{3,4},{4,5},{5,6},{6,7},{7,8},{8,9},{9,10},{10,1... | collective-permute-start | bytes 589832 | tf_op jit(solution)/shard_map/ppermute | solution.py:19
  378.2 2.1 collective-permute-done
  380.3 0.9 collective-permute-done.1
  381.2 0.4 fusion.31
  382.1 1.0 copy-done.2
  (86 shorter events, 3.3 us)
Async XLA Ops:
  0.6 0.7 copy-start
  351.4 20.1 %all-to-all-start = ((f32[8,3,4096]{2,1,0:T(4,128)}), f32[8,3,4096]{2,1,0:T(4,128)S(1)}, u32[]{:S(2)}, u32[]{:S(2)}) async-start(f32[8,3,4096]{2,1,0:T(4,128)} %reshape_reshape.3), calls=%async_computation | async-start | bytes 1048576 | tf_op jit(solution)/shard_map/all_to_all | solution.py:132
  361.9 10.6 %copy-start.1 = (f32[3,2,64,256]{3,2,1,0:T(8,128)S(1)}, f32[3,2,64,256]{3,2,1,0:T(8,128)}, u32[]{:S(2)}) copy-start(f32[3,2,64,256]{3,2,1,0:T(8,128)} %param.11) | copy-start | bytes 1179652
  372.9 7.4 %collective-permute-start = (f32[1,3,1,64,256]{4,3,2,1,0:T(8,128)S(1)}, f32[1,3,1,64,256]{4,3,2,1,0:T(8,128)S(1)}, u32[]{:S(2)}, u32[]{:S(2)}) collective-permute-start(f32[1,3,1,64,256]{4,3,2,1,0:T(8,128)S(1)} %get-tuple-element.276), channel_id=1, source_target_pairs={{1,0},{2,1},{3,2},{4,3},{5,4},{6,5},{7,6},{8,7},{9,8},{10,9},{11,1... | collective-permute-start | bytes 589832 | tf_op jit(solution)/shard_map/ppermute | solution.py:21
  374.2 7.0 %collective-permute-start.1 = (f32[1,3,1,64,256]{4,3,2,1,0:T(8,128)S(1)}, f32[1,3,1,64,256]{4,3,2,1,0:T(8,128)S(1)}, u32[]{:S(2)}, u32[]{:S(2)}) collective-permute-start(f32[1,3,1,64,256]{4,3,2,1,0:T(8,128)S(1)} %get-tuple-element.277), channel_id=1, source_target_pairs={{0,1},{1,2},{2,3},{3,4},{4,5},{5,6},{6,7},{7,8},{8,9},{9,10},{10,1... | collective-permute-start | bytes 589832 | tf_op jit(solution)/shard_map/ppermute | solution.py:19
  382.1 1.1 copy-start.2
where the time goes:
time: 389 us; the launch traced here: 383 us
  blocking collectives  256 us (66%)
  matrix products  85.3 us (22%)
  starting transfers between devices  15.9 us (4%)
  waiting for transfers between devices  12.5 us (3%)
  local copies, waits for them, and re-layouts  10.1 us (3%)
    all_gather x1, blocking collectives, body(): lax.all_gather(centre_positions, ('inst', 'space'), axis=1, tiled=True)  139 us
    all_gather x1, blocking collectives, body(): lax.all_gather(flat_moves, ('inst', 'space'), axis=1, tiled=True)  118 us
    dot_general x32, matrix products, add_block(): jnp.dot(piece_moves, tile, precision=lax.Precision.HIGHEST, preferred_ele...  84.4 us
    all_to_all x1, starting transfers between devices, body(): lax.all_to_all(summed.reshape(count_inst, 3, share), 'inst', split_axis=0...  10.6 us
    all_to_all x1, waiting for transfers between devices, body(): lax.all_to_all(summed.reshape(count_inst, 3, share), 'inst', split_axis=0...  9.5 us
  transfers between devices with their start and end apart: 3, of which 3 were waited for; matrix products, arithmetic and copies ran while one was open for 0% of the time, Pallas kernels for 0%

commit v1 on v0

v1 whole, which is shorter than its diff:
```python
import jax
import jax.numpy as jnp
from jax import lax
from jax.experimental import pallas as pl
from jax.experimental.pallas import tpu as pltpu
from jax.sharding import PartitionSpec as P

MESH = pl.DeviceIdType.MESH
HIGH = lax.Precision.HIGHEST
XS, YS, ZS, CORES = 4, 4, 16, 2
INST, SPACE = YS * CORES, XS * ZS
OWN = 8
BLOCKS = XS * YS * CORES
NC = BLOCKS * ZS * OWN
VALUES = 32
BINS = 16
CHUNK = 128
PLACED = 256
MARGIN = 1.0 + 2.0**-11
VMEM_LIMIT = 48 * 1024 * 1024


def vmem():
    return pl.BlockSpec(memory_space=pltpu.VMEM)


def params(**more):
    return pltpu.CompilerParams(vmem_limit_bytes=VMEM_LIMIT, **more)


def gather_kernel(amp_ref, coef_ref, pos_ref, out_ref, zbuf, send, recv):
    inst, space = lax.axis_index("inst"), lax.axis_index("space")
    y, core = inst // CORES, inst % CORES
    x, z = space // ZS, space % ZS
    z_peers = [(inst, x * ZS + lax.rem(z + k, ZS)) for k in range(1, ZS)]
    x_peers = [(inst, lax.rem(x + k, XS) * ZS + z) for k in range(1, XS)]
    y_peers = [(lax.rem(y + k, YS) * CORES + core, space) for k in range(1, YS)]
    other = [(y * CORES + (1 - core), space)]
    peers = z_peers + x_peers + y_peers + other
    barrier = pltpu.get_barrier_semaphore()
    for peer in peers:
        pl.semaphore_signal(barrier, inc=1, device_id=peer, device_id_type=MESH)

    amp = amp_ref[...]
    rows = [
        jnp.dot(amp, coef_ref[:, c, :], precision=HIGH, preferred_element_type=jnp.float32)
        for c in range(3)
    ]
    rows += [pos_ref[...], jnp.zeros((5, OWN), jnp.float32)]
    own = jnp.concatenate(rows, axis=0)
    own = jnp.concatenate([own, jnp.zeros((VALUES, 128 - OWN), jnp.float32)], axis=1)
    own = jnp.concatenate([own, jnp.zeros((128 - VALUES, 128), jnp.float32)], axis=0)
    own = own.T[0:OWN]
    row_id = lax.broadcasted_iota(jnp.int32, (OWN, 128), 0) % 4
    spread = jnp.zeros((OWN, 128), jnp.float32)
    for a in range(4):
        moved = own if a == 0 else pltpu.roll(own, VALUES * a, 1)
        spread = spread + jnp.where(row_id == a, moved, 0.0)
    zbuf[z] = jnp.concatenate(
        [
            jnp.sum(spread[0:4], axis=0, keepdims=True),
            jnp.sum(spread[4:8], axis=0, keepdims=True),
        ],
        axis=0,
    )
    pl.semaphore_wait(barrier, len(peers))

    def send_all(ref, targets, first):
        copies = []
        for k, peer in enumerate(targets):
            copy = pltpu.make_async_remote_copy(
                src_ref=ref,
                dst_ref=ref,
                send_sem=send.at[first + k],
                recv_sem=recv.at[first + k],
                device_id=peer,
                device_id_type=MESH,
            )
            copy.start()
            copies.append(copy)
        return copies

    copies = send_all(zbuf.at[z], z_peers, 0)
    for copy in copies:
        copy.wait()
    rows = jnp.concatenate([zbuf[i] for i in range(ZS)], axis=0)
    rows = jnp.concatenate([rows, jnp.zeros((128 - 2 * ZS, 128), jnp.float32)], axis=0).T
    block = rows[0:VALUES]
    for a in range(1, 4):
        block = block + pltpu.roll(rows[VALUES * a : VALUES * (a + 1)], VALUES * a, 1)
    row = core * (XS * YS) + y * XS
    out_ref[row + x] = block
    copies = send_all(out_ref.at[row + x], x_peers, ZS - 1)
    for copy in copies:
        copy.wait()
    copies = send_all(out_ref.at[pl.ds(row, XS)], y_peers, ZS + XS - 2)
    for copy in copies:
        copy.wait()
    copies = send_all(out_ref.at[pl.ds(core * (XS * YS), XS * YS)], other, ZS + XS + YS - 3)
    for copy in copies:
        copy.wait()


def gather(amplitudes, coefficients, positions):
    count = ZS + XS + YS - 2
    return pl.pallas_call(
        gather_kernel,
        out_shape=jax.ShapeDtypeStruct((BLOCKS, VALUES, 128), jnp.float32),
        in_specs=[vmem()] * 3,
        out_specs=vmem(),
        scratch_shapes=[
            pltpu.VMEM((ZS, 2, 128), jnp.float32),
            pltpu.SemaphoreType.DMA((count,)),
            pltpu.SemaphoreType.DMA((count,)),
        ],
        compiler_params=params(collective_id=0, has_side_effects=True),
        name="gather",
    )(amplitudes, coefficients, positions)


def whole_dot(a, b, dims=(((1,), (0,)), ((), ()))):
    return lax.dot_general(a, b, dims, preferred_element_type=jnp.float32)


def evaluate_kernel(place, g_ref, n_ref, moved_ref, deformed_ref, nodes, parts, order, weights, centres, ends):
    strip = place()
    first = pl.multiple_of(strip * 8, 8)
    base = []
    for c in range(3):
        for p in range(2):
            value = n_ref[c, p, pl.ds(first, 8), :]
            base.append(value)
            nodes[c, p] = value * 0.25

    spots = [g_ref[:, 24 + c, :] * 0.25 for c in range(3)]
    near = None
    for c in range(3):
        low = jnp.min(nodes[c]) - MARGIN
        high = jnp.max(nodes[c]) + MARGIN
        inside = (spots[c] >= low) & (spots[c] <= high)
        near = inside if near is None else near & inside
        if c == 1:
            j_low, scale = low, BINS / jnp.full((1, 1), high - low)

    def bin_of(value):
        return jnp.clip(jnp.floor((value - j_low) * scale), 0.0, BINS - 1.0)

    bins = jnp.where(near, bin_of(spots[1]), -1.0)

    member = jnp.concatenate(
        [(bins == float(b)).astype(jnp.float32) for b in range(BINS)], axis=0
    )
    short = member.astype(jnp.bfloat16)
    size = BINS * BLOCKS

    def less(shape, shift):
        return (
            lax.broadcasted_iota(jnp.int32, shape, 0) + shift
            <= lax.broadcasted_iota(jnp.int32, shape, 1)
        ).astype(jnp.float32).astype(jnp.bfloat16)

    before = whole_dot(short, less((128, 128), 0))
    totals = whole_dot(short, jnp.ones((128, 128), jnp.bfloat16))
    earlier = (
        lax.broadcasted_iota(jnp.int32, (size, size), 1)
        < lax.broadcasted_iota(jnp.int32, (size, size), 0)
    ).astype(jnp.float32).astype(jnp.bfloat16)
    offsets = whole_dot(earlier, totals.astype(jnp.bfloat16))
    placed = member * (before + offsets)
    position = placed[0:BLOCKS]
    for b in range(1, BINS):
        position = position + placed[b * BLOCKS : (b + 1) * BLOCKS]
    position = position - 1.0
    for i in range(BLOCKS // 2):
        order[i : i + 1, 0:128] = position[2 * i : 2 * i + 1]
        order[i : i + 1, 128:256] = position[2 * i + 1 : 2 * i + 2]
    found = jnp.max(position).astype(jnp.int32) + 1

    row_low = jnp.min(jnp.min(nodes[1], axis=0), axis=1, keepdims=True)
    row_high = jnp.max(jnp.max(nodes[1], axis=0), axis=1, keepdims=True)
    row_low, row_high = bin_of(row_low - MARGIN), bin_of(row_high + MARGIN)
    for j in range(8):
        start = jnp.sum(((bins >= 0.0) & (bins < row_low[j : j + 1])).astype(jnp.float32))
        stop = jnp.sum(((bins >= 0.0) & (bins <= row_high[j : j + 1])).astype(jnp.float32))
        ends[0, j] = start.astype(jnp.int32) // CHUNK
        ends[1, j] = (stop.astype(jnp.int32) + (CHUNK - 1)) // CHUNK

    def split(i, carry):
        for half in range(2):
            value = g_ref[2 * i + half]
            motion = value[0:24]
            top = motion.astype(jnp.bfloat16).astype(jnp.float32)
            spot = value[24:32] * 0.25
            one = spot.astype(jnp.bfloat16).astype(jnp.float32)
            two = (spot - one).astype(jnp.bfloat16).astype(jnp.float32)
            three = spot - one - two
            parts[i, :, half * 128 : half * 128 + 128] = jnp.concatenate(
                [top, motion - top, one, two, three, jnp.zeros((8, 128), jnp.float32)], axis=0
            ).astype(jnp.bfloat16)
        return carry

    lax.fori_loop(0, BLOCKS // 2, split, 0)

    slot = lax.broadcasted_iota(jnp.int32, (PLACED, 256), 0).astype(jnp.float32)

    def place_chunk(s, carry):
        begin = (s * PLACED).astype(jnp.float32)
        total = jnp.zeros((80, PLACED), jnp.float32)
        for i in range(BLOCKS // 2):
            hit = (slot == (order[i : i + 1, :] - begin)).astype(jnp.float32).astype(jnp.bfloat16)
            total = total + whole_dot(parts[i], hit, (((1,), (1,)), ((), ())))
        short = total[0:48].astype(jnp.bfloat16)
        weights[2 * s] = short[:, 0:128]
        weights[2 * s + 1] = short[:, 128:256]
        spot = (total[48:56] + total[56:64]) + total[64:72]
        for half in range(2):
            piece = jnp.concatenate(
                [spot[:, half * 128 : half * 128 + 128], jnp.zeros((120, 128), jnp.float32)], axis=0
            ).T
            at = pl.multiple_of(s * PLACED + half * 128, 128)
            for c in range(3):
                centres[c, pl.ds(at, 128), :] = jnp.broadcast_to(piece[:, c : c + 1], (128, 128))
        return carry

    lax.fori_loop(0, (found + (PLACED - 1)) // PLACED, place_chunk, 0)

    for j in range(8):

        def add(chunk, sums, j=j):
            at = pl.multiple_of(chunk * CHUNK, CHUNK)
            spot = [centres[c, pl.ds(at, CHUNK), :] for c in range(3)]
            pieces = weights[chunk]
            result = []
            for p in range(2):
                tops, rests = [], []
                for half in range(2):
                    square = None
                    for c in range(3):
                        gap = spot[c] - nodes[c, p, j : j + 1, half * 128 : half * 128 + 128]
                        square = gap * gap if square is None else square + gap * gap
                    radius = square * lax.rsqrt(jnp.maximum(square, 1e-30))
                    rest = jnp.maximum(1.0 - radius, 0.0)
                    rest = rest * rest
                    value = rest * rest * (4.0 * radius + 1.0)
                    top = value.astype(jnp.bfloat16)
                    tops.append(top)
                    rests.append((value - top.astype(jnp.float32)).astype(jnp.bfloat16))
                full = whole_dot(pieces, jnp.concatenate(tops, axis=1))
                extra = whole_dot(pieces[0:32], jnp.concatenate(rests, axis=1))
                result.append(sums[p] + (full[0:24] + (full[24:48] + extra[0:24])))
            return tuple(result)

        zero = jnp.zeros((24, 256), jnp.float32)
        sums = lax.fori_loop(ends[0, j], ends[1, j], add, (zero, zero))
        for p in range(2):
            for c in range(3):
                value = sums[p][c * 8 : c * 8 + 8]
                moved_ref[:, c, p, j, :] = value
                deformed_ref[:, c, p, j, :] = value + base[2 * c + p][j : j + 1]


def evaluate(gathered, base_nodes, place):
    shape = jax.ShapeDtypeStruct((INST, 3, 2, 8, 256), jnp.float32)
    return pl.pallas_call(
        lambda *refs: evaluate_kernel(place, *refs),
        out_shape=(shape, shape),
        in_specs=[vmem()] * 2,
        out_specs=(vmem(), vmem()),
        scratch_shapes=[
            pltpu.VMEM((3, 2, 8, 256), jnp.float32),
            pltpu.VMEM((BLOCKS // 2, 80, 256), jnp.bfloat16),
            pltpu.VMEM((BLOCKS // 2, 256), jnp.float32),
            pltpu.VMEM((NC // CHUNK, 48, CHUNK), jnp.bfloat16),
            pltpu.VMEM((3, NC, 128), jnp.float32),
            pltpu.SMEM((2, 8), jnp.int32),
        ],
        compiler_params=params(),
        name="evaluate",
    )(gathered, base_nodes)


def shifted(value, axis):
    extent = value.shape[axis]
    at = lax.broadcasted_iota(jnp.int32, value.shape, axis)
    following = pltpu.roll(value, extent - 1, axis)
    preceding = pltpu.roll(value, 1, axis)
    upper = jnp.where(at == extent - 1, 2.0 * value - preceding, following)
    lower = jnp.where(at == 0, 2.0 * value - following, preceding)
    return (upper - lower) * 0.5


def cross(a, b):
    return [
        a[1] * b[2] - a[2] * b[1],
        a[2] * b[0] - a[0] * b[2],
        a[0] * b[1] - a[1] * b[0],
    ]


def exchange_kernel(moved_ref, deformed_ref, n_ref, disp_ref, metrics_ref, halo, send, recv, local):
    inst, space = lax.axis_index("inst"), lax.axis_index("space")
    behind, ahead = lax.rem(space + SPACE - 1, SPACE), lax.rem(space + 1, SPACE)
    barrier = pltpu.get_barrier_semaphore()
    targets = [lax.rem(inst + k, INST) for k in range(INST)]
    peers = [(t, s) for t in targets for s in (behind, ahead)] + [(t, space) for t in targets[1:]]
    for peer in peers:
        pl.semaphore_signal(barrier, inc=1, device_id=peer, device_id_type=MESH)
    pl.semaphore_wait(barrier, len(peers))
    rows = pl.ds(pl.multiple_of(inst * 8, 8), 8)
    copies = []

    def start(source, target, kind, k, device):
        copy = pltpu.make_async_remote_copy(
            src_ref=source,
            dst_ref=target,
            send_sem=send.at[kind, k],
            recv_sem=recv.at[kind, k],
            device_id=device,
            device_id_type=MESH,
        )
        copy.start()
        copies.append(copy)

    for k, t in enumerate(targets):
        start(deformed_ref.at[t, :, 0], halo.at[1, :, rows, :], 0, k, (t, behind))
        start(deformed_ref.at[t, :, 1], halo.at[0, :, rows, :], 1, k, (t, ahead))
        if k:
            start(moved_ref.at[t], disp_ref.at[0, :, :, rows, :], 2, k, (t, space))
    mine = pltpu.make_async_copy(moved_ref.at[inst], disp_ref.at[0, :, :, rows, :], local)
    mine.start()
    mine.wait()
    for copy in copies:
        copy.wait()
    for p in range(2):
        here = [n_ref[c, p] + disp_ref[0, c, p] for c in range(3)]
        there = [n_ref[c, 1 - p] + disp_ref[0, c, 1 - p] for c in range(3)]
        along_i = []
        for c in range(3):
            if p == 0:
                beyond = jnp.where(space == 0, 2.0 * here[c] - there[c], halo[0, c])
                along_i.append((there[c] - beyond) * 0.5)
            else:
                beyond = jnp.where(space == SPACE - 1, 2.0 * here[c] - there[c], halo[1, c])
                along_i.append((beyond - there[c]) * 0.5)
        along_j = [shifted(value, 0) for value in here]
        along_k = [shifted(value, 1) for value in here]
        one = cross(along_j, along_k)
        for c in range(3):
            metrics_ref[0, c, p] = one[c]
        metrics_ref[0, 9, p] = along_i[0] * one[0] + along_i[1] * one[1] + along_i[2] * one[2]
        two = cross(along_k, along_i)
        for c in range(3):
            metrics_ref[0, 3 + c, p] = two[c]
        three = cross(along_i, along_j)
        for c in range(3):
            metrics_ref[0, 6 + c, p] = three[c]


def exchange(moved, deformed, base_nodes):
    return pl.pallas_call(
        exchange_kernel,
        out_shape=(
            jax.ShapeDtypeStruct((1,) + base_nodes.shape, jnp.float32),
            jax.ShapeDtypeStruct((1, 10) + base_nodes.shape[1:], jnp.float32),
        ),
        in_specs=[vmem()] * 3,
        out_specs=(vmem(), vmem()),
        scratch_shapes=[
            pltpu.VMEM((2, 3) + base_nodes.shape[2:], jnp.float32),
            pltpu.SemaphoreType.DMA((3, INST)),
            pltpu.SemaphoreType.DMA((3, INST)),
            pltpu.SemaphoreType.DMA,
        ],
        compiler_params=params(collective_id=1, has_side_effects=True),
        name="exchange",
    )(moved, deformed, base_nodes)


def body(amplitudes, modal_coeffs, centre_positions, base_nodes):
    gathered = gather(amplitudes, modal_coeffs, centre_positions)
    moved, deformed = evaluate(gathered, base_nodes, lambda: lax.axis_index("inst"))
    return exchange(moved, deformed, base_nodes)


def solution(mesh):
    in_specs = (
        P(),
        P(None, None, ("inst", "space")),
        P(None, ("inst", "space")),
        P(None, "space", None, None),
    )
    out_specs = (P("inst", None, "space", None, None), P("inst", None, "space", None, None))
    return jax.shard_map(body, mesh=mesh, in_specs=in_specs, out_specs=out_specs, check_vma=False)
```

time: 389 us -> 72.2 us (0.19)
  the two profiles are of different devices: /device:TPU:1 before, /device:TPU:3 now
where the time goes in v1:
time: 72.2 us; the launch traced here: 72 us
  Pallas kernels  66.3 us (92%)
  local copies, waits for them, and re-layouts  4.95 us (7%)
    pallas_call x1, Pallas kernels, gather(): pl.pallas_call(gather_kernel, out_shape=jax.ShapeDtypeStruct((BLOCKS, VAL...  32.3 us
    pallas_call x1, Pallas kernels, exchange(): pl.pallas_call(exchange_kernel, out_shape=(jax.ShapeDtypeStruct((1,) + ba...  17.4 us
    pallas_call x1, Pallas kernels, evaluate(): pl.pallas_call(lambda *refs: evaluate_kernel(place, *refs), out_shape=(sh...  16.6 us
    unnamed x9, local copies, waits for them, and re-layouts  4.95 us

profile of v1, /device:TPU:3, one launch (start us, length us, event | category | flops | bytes accessed | tf_op | source)
XLA Modules:
  0.0 72.0 jit_solution(17535603125038633711)
XLA Ops:
  0.6 0.8 %copy.6.coef_ref = f32[40,3,8]{2,1,0:T(4,128)S(1)} copy(f32[40,3,8]{0,2,1:T(8,128)} %param.5) | data formatting | bytes 7680 | tf_op args[1]
  1.4 0.0 copy-start.1
  1.4 0.7 copy-done.1
  2.1 0.0 copy-start.2
  2.1 0.7 copy-done.2
  2.8 32.3 %gather.1.refs_0_ = f32[32,32,128]{2,1,0:T(8,128)S(1)} custom-call(f32[8,40]{1,0:T(8,128)S(1)} %copy-done.1, f32[40,3,8]{2,1,0:T(4,128)S(1)} %copy.6.coef_ref, f32[3,8]{1,0:T(4,128)S(1)} %copy-done.2), custom_call_target="tpu_custom_call" | custom-call | tf_op jit(solution)/shard_map/gather/pallas_call | solution.py:106
  35.1 0.0 copy-start
  35.1 1.0 %copy-done = f32[3,2,64,256]{3,2,1,0:T(8,128)S(1)} copy-done((f32[3,2,64,256]{3,2,1,0:T(8,128)S(1)}, f32[3,2,64,256]{3,2,1,0:T(8,128)}, u32[]{:S(2)}) %copy-start) | copy-done | bytes 393240
  36.1 16.6 %evaluate.1 = (f32[8,3,2,8,256]{4,3,2,1,0:T(8,128)S(1)}, f32[8,3,2,8,256]{4,3,2,1,0:T(8,128)S(1)}) custom-call(f32[32,32,128]{2,1,0:T(8,128)S(1)} %gather.1.refs_0_, f32[3,2,64,256]{3,2,1,0:T(8,128)S(1)} %copy-done), custom_call_target="tpu_custom_call" | custom-call | tf_op jit(solution)/shard_map/evaluate/pallas_call | solution.py:264
  52.7 17.4 %exchange.1 = (f32[1,3,2,64,256]{4,3,2,1,0:T(8,128)S(1)}, f32[1,10,2,64,256]{4,3,2,1,0:T(8,128)S(1)}) custom-call(f32[8,3,2,8,256]{4,3,2,1,0:T(8,128)S(1)} %get-tuple-element.4.moved_ref, f32[8,3,2,8,256]{4,3,2,1,0:T(8,128)S(1)} %get-tuple-element.5.deformed_ref, f32[3,2,64,256]{3,2,1,0:T(8,128)S(1)} %copy-done), custom_call_target="tpu_custom_call" | custom-call | tf_op jit(solution)/shard_map/exchange/pallas_call | solution.py:360
  70.1 0.7 %copy.9 = f32[1,3,2,64,256]{4,3,2,1,0:T(8,128)} copy(f32[1,3,2,64,256]{4,3,2,1,0:T(8,128)S(1)} %get-tuple-element.8) | data formatting | bytes 786432
  70.9 1.1 %copy.10 = f32[1,10,2,64,256]{4,3,2,1,0:T(8,128)} copy(f32[1,10,2,64,256]{4,3,2,1,0:T(8,128)S(1)} %get-tuple-element.9) | data formatting | bytes 2621440
Async XLA Ops:
  1.4 0.7 copy-start.1
  2.1 0.7 copy-start.2
  35.1 1.0 %copy-start = (f32[3,2,64,256]{3,2,1,0:T(8,128)S(1)}, f32[3,2,64,256]{3,2,1,0:T(8,128)}, u32[]{:S(2)}) copy-start(f32[3,2,64,256]{3,2,1,0:T(8,128)} %n_ref.1) | copy-start | bytes 1179652

commit v2 on v1

v2 whole, which is shorter than its diff:
```python
import jax
import jax.numpy as jnp
from jax import lax
from jax.experimental import pallas as pl
from jax.experimental.pallas import tpu as pltpu
from jax.sharding import PartitionSpec as P

MESH = pl.DeviceIdType.MESH
HIGH = lax.Precision.HIGHEST
XS, YS, ZS, CORES = 4, 4, 16, 2
INST, SPACE = YS * CORES, XS * ZS
OWN = 8
BLOCKS = XS * YS * CORES
NC = BLOCKS * ZS * OWN
VALUES = 32
BINS = 32
CHUNK = 128
PLACED = 256
MARGIN = 1.0 + 2.0**-11
VMEM_LIMIT = 48 * 1024 * 1024


def vmem():
    return pl.BlockSpec(memory_space=pltpu.VMEM)


def params(**more):
    return pltpu.CompilerParams(vmem_limit_bytes=VMEM_LIMIT, **more)


def swap_blocks(arrays):
    block = lax.broadcasted_iota(jnp.int32, arrays[0].shape, 1) // 16
    arrays = list(arrays)
    for step in (1, 2, 4):
        upper = (block & step) != 0
        for a in range(8):
            if not a & step:
                one, two = arrays[a], arrays[a | step]
                arrays[a] = jnp.where(upper, pltpu.roll(two, 16 * step, 1), one)
                arrays[a | step] = jnp.where(upper, two, pltpu.roll(one, 128 - 16 * step, 1))
    return arrays


def gather_kernel(own_ref, strip, out_ref, tiles, zbuf, send, recv):
    inst, space = lax.axis_index("inst"), lax.axis_index("space")
    y, core = inst // CORES, inst % CORES
    x, z = space // ZS, space % ZS
    z_peers = [(inst, x * ZS + lax.rem(z + k, ZS)) for k in range(1, ZS)]
    steps = [(a, b) for a in range(YS) for b in range(XS) if a or b]
    plane_peers = [
        (lax.rem(y + a, YS) * CORES + core, lax.rem(x + b, XS) * ZS + z) for a, b in steps
    ]
    other = (y * CORES + (1 - core), space)
    peers = z_peers + plane_peers + [other]
    barrier = pltpu.get_barrier_semaphore()
    for peer in peers:
        pl.semaphore_signal(barrier, inc=1, device_id=peer, device_id_type=MESH)

    transposed = (((1,), (1,)), ((), ()))

    def high_dot(a, b):
        return lax.dot_general(a, b, transposed, precision=HIGH, preferred_element_type=jnp.float32)

    amp = own_ref[24:32]
    eye = (
        lax.broadcasted_iota(jnp.int32, (OWN, OWN), 0) == lax.broadcasted_iota(jnp.int32, (OWN, OWN), 1)
    ).astype(jnp.float32)
    own = [high_dot(own_ref[8 * c : 8 * c + 8], amp) for c in range(3)]
    own.append(high_dot(eye, own_ref[32:40, 0:OWN])[:, 0:3])
    own = jnp.concatenate(own + [jnp.zeros((OWN, 128 - 27), jnp.float32)], axis=1)
    row_id = lax.broadcasted_iota(jnp.int32, (OWN, 128), 0) % 4
    spread = jnp.zeros((OWN, 128), jnp.float32)
    for a in range(4):
        moved = own if a == 0 else pltpu.roll(own, VALUES * a, 1)
        spread = spread + jnp.where(row_id == a, moved, 0.0)
    zbuf[z] = jnp.concatenate(
        [
            jnp.sum(spread[0:4], axis=0, keepdims=True),
            jnp.sum(spread[4:8], axis=0, keepdims=True),
        ],
        axis=0,
    )

    for half in range(2):
        lanes = slice(half * 128, half * 128 + 128)
        rows = [
            jnp.concatenate(
                [strip[c, p, j : j + 1, lanes] for c in range(3) for p in range(2)]
                + [jnp.zeros((2, 128), jnp.float32)],
                axis=0,
            )
            for j in range(8)
        ]
        for t, tile in enumerate(swap_blocks(rows)):
            tiles[8 * half + t] = tile * 0.25
    pl.semaphore_wait(barrier, len(peers))

    def start(ref, k, peer):
        copy = pltpu.make_async_remote_copy(
            src_ref=ref,
            dst_ref=ref,
            send_sem=send.at[k],
            recv_sem=recv.at[k],
            device_id=peer,
            device_id_type=MESH,
        )
        copy.start()
        return copy

    far_first = sorted(range(ZS - 1), key=lambda k: -min(k + 1, ZS - 1 - k))
    copies = [start(zbuf.at[z], k, z_peers[k]) for k in far_first]
    for copy in reversed(copies):
        copy.wait()
    rows = jnp.concatenate([zbuf[i] for i in range(ZS)], axis=0)
    rows = jnp.concatenate([rows, jnp.zeros((128 - 2 * ZS, 128), jnp.float32)], axis=0).T
    block = rows[0:VALUES]
    for a in range(1, 4):
        block = block + pltpu.roll(rows[VALUES * a : VALUES * (a + 1)], VALUES * a, 1)
    mine = core * (XS * YS) + y * XS + x
    out_ref[mine] = block

    def hops(k):
        a, b = steps[k]
        return min(a, YS - a) + min(b, XS - b)

    far_first = sorted(range(len(steps)), key=lambda k: -hops(k))
    copies = [start(out_ref.at[mine], ZS - 1 + k, plane_peers[k]) for k in far_first]
    passed = [start(out_ref.at[mine], ZS - 1 + len(steps), other)]
    for copy, k in reversed(list(zip(copies, far_first))):
        copy.wait_recv()
        a, b = steps[k]
        origin = core * (XS * YS) + lax.rem(y + YS - a, YS) * XS + lax.rem(x + XS - b, XS)
        passed.append(start(out_ref.at[origin], ZS + len(steps) + k, other))
    for copy in copies:
        copy.wait_send()
    for copy in passed:
        copy.wait()


def gather(own, strip):
    count = ZS + 2 * XS * YS - 2
    return pl.pallas_call(
        gather_kernel,
        out_shape=(
            jax.ShapeDtypeStruct((BLOCKS, VALUES, 128), jnp.float32),
            jax.ShapeDtypeStruct((16, 8, 128), jnp.float32),
        ),
        in_specs=[vmem()] * 2,
        out_specs=(vmem(), vmem()),
        scratch_shapes=[
            pltpu.VMEM((ZS, 2, 128), jnp.float32),
            pltpu.SemaphoreType.DMA((count,)),
            pltpu.SemaphoreType.DMA((count,)),
        ],
        compiler_params=params(collective_id=0, has_side_effects=True),
        name="gather",
    )(own, strip)


def whole_dot(a, b, precision=None):
    return jnp.dot(a, b, precision=precision, preferred_element_type=jnp.float32)


def evaluate_kernel(g_ref, strip, tiles, moved_ref, deformed_ref, nodes, parts, order, weights, centres, found, edges, ends, arrived):
    nodes[...] = strip[...] * 0.25

    spots = [g_ref[:, 24 + c, :] * 0.25 for c in range(3)]
    near = None
    for c in range(3):
        low = jnp.min(nodes[c]) - MARGIN
        high = jnp.max(nodes[c]) + MARGIN
        inside = (spots[c] >= low) & (spots[c] <= high)
        near = inside if near is None else near & inside
        if c == 2:
            k_low, scale = low, BINS / jnp.full((1, 1), high - low)

    def bin_of(value):
        return jnp.clip(jnp.floor((value - k_low) * scale), 0.0, BINS - 1.0)

    bins = jnp.where(near, bin_of(spots[2]), -1.0)

    bin_id = lax.broadcasted_iota(jnp.int32, (BINS, 128), 0).astype(jnp.float32)
    member = jnp.concatenate(
        [(bins[i : i + 1] == bin_id).astype(jnp.float32) for i in range(BLOCKS)], axis=0
    )
    lane = lax.broadcasted_iota(jnp.int32, (128, 256), 1)
    counting = ((lax.broadcasted_iota(jnp.int32, (128, 256), 0) <= lane) | (lane >= 128)).astype(jnp.float32)
    counts = whole_dot(member.astype(jnp.bfloat16), counting.astype(jnp.bfloat16))
    total = counts[0:BINS, 128:256]
    for i in range(1, BLOCKS):
        total = total + counts[i * BINS : (i + 1) * BINS, 128:256]
    earlier = (
        lax.broadcasted_iota(jnp.int32, (BINS, BINS), 1) < lax.broadcasted_iota(jnp.int32, (BINS, BINS), 0)
    ).astype(jnp.float32)
    running = whole_dot(earlier, total, HIGH)
    rows = []
    for i in range(BLOCKS):
        own = slice(i * BINS, (i + 1) * BINS)
        rows.append(jnp.sum(member[own] * (running + counts[own, 0:128]), axis=0, keepdims=True) - 1.0)
        running = running + counts[own, 128:256]
    position = jnp.concatenate(rows + [jnp.zeros((128 - BLOCKS, 128), jnp.float32)], axis=0).T
    for i in range(BLOCKS):
        order[i * 128 : i * 128 + 128, :] = jnp.broadcast_to(position[:, i : i + 1], (128, 128))

    k_min = jnp.min(jnp.min(nodes[2], axis=0), axis=0, keepdims=True)
    k_max = jnp.max(jnp.max(nodes[2], axis=0), axis=0, keepdims=True)
    for step in (1, 2, 4, 8):
        k_min = jnp.minimum(k_min, pltpu.roll(k_min, step, 1))
        k_max = jnp.maximum(k_max, pltpu.roll(k_max, step, 1))
    wide_id = lax.broadcasted_iota(jnp.int32, (BINS, 256), 0).astype(jnp.float32)
    wide_total = jnp.concatenate([total, total], axis=1)
    start = jnp.sum(jnp.where(wide_id < bin_of(k_min - MARGIN), wide_total, 0.0), axis=0, keepdims=True)
    stop = jnp.sum(jnp.where(wide_id <= bin_of(k_max + MARGIN), wide_total, 0.0), axis=0, keepdims=True)
    edges[0:1, :] = jnp.floor(start * (1.0 / CHUNK)).astype(jnp.int32)
    edges[1:2, :] = jnp.floor((stop + (CHUNK - 1.0)) * (1.0 / CHUNK)).astype(jnp.int32)
    edges[2:3, :] = jnp.floor(
        (jnp.sum(wide_total, axis=0, keepdims=True) + (PLACED - 1.0)) * (1.0 / PLACED)
    ).astype(jnp.int32)
    copy = pltpu.make_async_copy(edges, ends, arrived)
    copy.start()

    def split(i, carry):
        for half in range(2):
            value = g_ref[2 * i + half]
            motion = value[0:24]
            top = motion.astype(jnp.bfloat16).astype(jnp.float32)
            spot = value[24:32] * 0.25
            one = spot.astype(jnp.bfloat16).astype(jnp.float32)
            two = (spot - one).astype(jnp.bfloat16).astype(jnp.float32)
            three = spot - one - two
            parts[i, :, half * 128 : half * 128 + 128] = jnp.concatenate(
                [top, motion - top, one, two, three, jnp.zeros((8, 128), jnp.float32)], axis=0
            ).astype(jnp.bfloat16)
        return carry

    lax.fori_loop(0, BLOCKS // 2, split, 0)
    copy.wait()

    slot = lax.broadcasted_iota(jnp.int32, (1, 128), 1)

    def place_chunk(s, carry):
        sums = jnp.zeros((80, PLACED), jnp.float32)
        wanted = [(slot + (s * PLACED + 128 * half)).astype(jnp.float32) for half in range(2)]
        for i in range(BLOCKS // 2):
            at = order[i * 256 : i * 256 + 256, :]
            hit = jnp.concatenate([(at == w).astype(jnp.float32) for w in wanted], axis=1)
            sums = sums + whole_dot(parts[i], hit.astype(jnp.bfloat16))
        short = sums[0:48].astype(jnp.bfloat16)
        spot = (sums[48:56] + sums[56:64]) + sums[64:72]
        for half in range(2):
            lanes = slice(half * 128, half * 128 + 128)
            weights[2 * s + half] = short[:, lanes]
            piece = jnp.concatenate([spot[:, lanes], jnp.zeros((120, 128), jnp.float32)], axis=0).T
            at = pl.multiple_of(s * PLACED + half * 128, 128)
            for c in range(3):
                centres[c, pl.ds(at, 128), :] = jnp.broadcast_to(piece[:, c : c + 1], (128, 128))
        return carry

    lax.fori_loop(0, ends[2, 0], place_chunk, 0)

    for t in range(16):

        def add(chunk, sums, t=t):
            at = pl.multiple_of(chunk * CHUNK, CHUNK)
            spot = [centres[c, pl.ds(at, CHUNK), :] for c in range(3)]
            pieces = weights[chunk]
            tops, rests = [], []
            for p in range(2):
                square = None
                for c in range(3):
                    gap = spot[c] - tiles[t, 2 * c + p : 2 * c + p + 1, :]
                    square = gap * gap if square is None else square + gap * gap
                radius = square * lax.rsqrt(jnp.maximum(square, 1e-30))
                rest = jnp.maximum(1.0 - radius, 0.0)
                rest = rest * rest
                value = rest * rest * (4.0 * radius + 1.0)
                top = value.astype(jnp.bfloat16)
                tops.append(top)
                rests.append((value - top.astype(jnp.float32)).astype(jnp.bfloat16))
            full = whole_dot(pieces, jnp.concatenate(tops, axis=1))
            extra = whole_dot(pieces[0:32], jnp.concatenate(rests, axis=1))
            return sums + (full[0:24] + (full[24:48] + extra[0:24]))

        last = 16 * t + 15
        found[t] = lax.fori_loop(ends[0, last], ends[1, last], add, jnp.zeros((24, 256), jnp.float32))

    for p in range(2):
        for half in range(2):
            lanes = slice(half * 128, half * 128 + 128)
            rows = swap_blocks([found[8 * half + t, :, p * 128 : p * 128 + 128] for t in range(8)])
            for j in range(8):
                for c in range(3):
                    value = rows[j][c * 8 : c * 8 + 8]
                    into = pl.ds(c * 32 + p * 16 + half * 8 + j, 8, stride=96)
                    moved_ref[into, :] = value
                    deformed_ref[into, :] = value + strip[c, p, j : j + 1, lanes]


def evaluate(gathered, strip, tiles):
    shape = jax.ShapeDtypeStruct((INST * 96, 128), jnp.float32)
    results = pl.pallas_call(
        evaluate_kernel,
        out_shape=(shape, shape),
        in_specs=[vmem()] * 3,
        out_specs=(vmem(), vmem()),
        scratch_shapes=[
            pltpu.VMEM((3, 2, 8, 256), jnp.float32),
            pltpu.VMEM((BLOCKS // 2, 80, 256), jnp.bfloat16),
            pltpu.VMEM((NC, 128), jnp.float32),
            pltpu.VMEM((NC // CHUNK, 48, CHUNK), jnp.bfloat16),
            pltpu.VMEM((3, NC, 128), jnp.float32),
            pltpu.VMEM((16, 24, 256), jnp.float32),
            pltpu.VMEM((8, 256), jnp.int32),
            pltpu.SMEM((8, 256), jnp.int32),
            pltpu.SemaphoreType.DMA,
        ],
        compiler_params=params(),
        name="evaluate",
    )(gathered, strip, tiles)
    return [value.reshape(INST, 3, 2, 2, 8, 128) for value in results]


def exchange_kernel(moved_ref, deformed_ref, own, halo, send, recv, local):
    inst, space = lax.axis_index("inst"), lax.axis_index("space")
    behind, ahead = lax.rem(space + SPACE - 1, SPACE), lax.rem(space + 1, SPACE)
    barrier = pltpu.get_barrier_semaphore()
    targets = [lax.rem(inst + k, INST) for k in range(INST)]
    peers = [(t, s) for t in targets for s in (behind, ahead)] + [(t, space) for t in targets[1:]]
    for peer in peers:
        pl.semaphore_signal(barrier, inc=1, device_id=peer, device_id_type=MESH)
    rows = pl.ds(pl.multiple_of(inst * 8, 8), 8)
    stays = pltpu.make_async_copy(moved_ref.at[inst], own.at[:, :, :, rows, :], local)
    stays.start()
    pl.semaphore_wait(barrier, len(peers))
    copies = []

    def start(source, target, kind, k, device):
        copy = pltpu.make_async_remote_copy(
            src_ref=source,
            dst_ref=target,
            send_sem=send.at[kind, k],
            recv_sem=recv.at[kind, k],
            device_id=device,
            device_id_type=MESH,
        )
        copy.start()
        copies.append(copy)

    for k in (4, 3, 5, 2, 6, 1, 7, 0):
        t = targets[k]
        start(deformed_ref.at[t, :, 0], halo.at[1, :, :, rows, :], 0, k, (t, behind))
        start(deformed_ref.at[t, :, 1], halo.at[0, :, :, rows, :], 1, k, (t, ahead))
        if k:
            start(moved_ref.at[t], own.at[:, :, :, rows, :], 2, k, (t, space))
    for copy in [stays] + copies:
        copy.wait()


def exchange(moved, deformed, rows, width):
    return pl.pallas_call(
        exchange_kernel,
        out_shape=(
            jax.ShapeDtypeStruct((3, 2, 2, rows, width), jnp.float32),
            jax.ShapeDtypeStruct((2, 3, 2, rows, width), jnp.float32),
        ),
        in_specs=[vmem(), vmem()],
        out_specs=(vmem(), vmem()),
        scratch_shapes=[
            pltpu.SemaphoreType.DMA((3, INST)),
            pltpu.SemaphoreType.DMA((3, INST)),
            pltpu.SemaphoreType.DMA,
        ],
        compiler_params=params(collective_id=1, has_side_effects=True),
        name="exchange",
    )(moved, deformed)


def shifted(value, axis):
    extent = value.shape[axis]
    at = lax.broadcasted_iota(jnp.int32, value.shape, axis)
    following = pltpu.roll(value, extent - 1, axis)
    preceding = pltpu.roll(value, 1, axis)
    upper = jnp.where(at == extent - 1, 2.0 * value - preceding, following)
    lower = jnp.where(at == 0, 2.0 * value - following, preceding)
    return (upper - lower) * 0.5


def cross(a, b):
    return [
        a[1] * b[2] - a[2] * b[1],
        a[2] * b[0] - a[0] * b[2],
        a[0] * b[1] - a[1] * b[0],
    ]


def metrics_kernel(own, halo, n_ref, disp_hbm, metrics_hbm, disp, metrics, sems):
    space = lax.axis_index("space")
    copies = []

    def leave(source, target):
        copy = pltpu.make_async_copy(source, target, sems.at[len(copies)])
        copy.start()
        copies.append(copy)

    for c in range(3):
        for p in range(2):
            for half in range(2):
                disp[c, p, :, half * 128 : half * 128 + 128] = own[c, p, half]
    leave(disp, disp_hbm.at[0])

    def beside(which, c):
        return jnp.concatenate([halo[which, c, 0], halo[which, c, 1]], axis=1)

    for p in range(2):
        here = [n_ref[c, p] + disp[c, p] for c in range(3)]
        there = [n_ref[c, 1 - p] + disp[c, 1 - p] for c in range(3)]
        along_i = []
        for c in range(3):
            if p == 0:
                beyond = jnp.where(space == 0, 2.0 * here[c] - there[c], beside(0, c))
                along_i.append((there[c] - beyond) * 0.5)
            else:
                beyond = jnp.where(space == SPACE - 1, 2.0 * here[c] - there[c], beside(1, c))
                along_i.append((beyond - there[c]) * 0.5)
        along_j = [shifted(value, 0) for value in here]
        along_k = [shifted(value, 1) for value in here]
        one = cross(along_j, along_k)
        two = cross(along_k, along_i)
        three = cross(along_i, along_j)
        last = along_i[0] * one[0] + along_i[1] * one[1] + along_i[2] * one[2]
        for row, value in enumerate(one + two + three + [last]):
            metrics[p, row] = value
        leave(metrics.at[p], metrics_hbm.at[0, :, p])
    for copy in copies:
        copy.wait()


def metric_rows(own, halo, base_nodes):
    anywhere = pl.BlockSpec(memory_space=pltpu.HBM)
    return pl.pallas_call(
        metrics_kernel,
        out_shape=(
            jax.ShapeDtypeStruct((1,) + base_nodes.shape, jnp.float32),
            jax.ShapeDtypeStruct((1, 10) + base_nodes.shape[1:], jnp.float32),
        ),
        in_specs=[vmem()] * 3,
        out_specs=(anywhere, anywhere),
        scratch_shapes=[
            pltpu.VMEM(base_nodes.shape, jnp.float32),
            pltpu.VMEM((2, 10) + base_nodes.shape[2:], jnp.float32),
            pltpu.SemaphoreType.DMA((3,)),
        ],
        compiler_params=params(),
        name="metrics",
    )(own, halo, base_nodes)


def body(amplitudes, modal_coeffs, centre_positions, base_nodes):
    modes = amplitudes.shape[1]
    own = jnp.concatenate(
        [
            modal_coeffs.transpose(1, 2, 0).reshape(3 * OWN, modes),
            amplitudes,
            jnp.pad(centre_positions, ((0, 5), (0, modes - OWN))),
        ],
        axis=0,
    )
    strip = lax.dynamic_slice_in_dim(base_nodes, lax.axis_index("inst") * 8, 8, 2)
    gathered, tiles = gather(own, strip)
    moved, deformed = evaluate(gathered, strip, tiles)
    rows, width = base_nodes.shape[2], base_nodes.shape[3] // 2
    own, halo = exchange(moved, deformed, rows, width)
    return metric_rows(own, halo, base_nodes)


def solution(mesh):
    in_specs = (
        P(),
        P(None, None, ("inst", "space")),
        P(None, ("inst", "space")),
        P(None, "space", None, None),
    )
    out_specs = (P("inst", None, "space", None, None), P("inst", None, "space", None, None))
    return jax.shard_map(body, mesh=mesh, in_specs=in_specs, out_specs=out_specs, check_vma=False)
```

time: 72.2 us -> 58.8 us (0.81)
  the two profiles are of different devices: /device:TPU:3 before, /device:TPU:6 now
where the time goes in v2:
time: 58.8 us; the launch traced here: 58.5 us
  Pallas kernels  56.2 us (96%)
  local copies, waits for them, and re-layouts  0.81 us (1%)
  other arithmetic  0.79 us (1%)
  between operations  0.68 us (1%)
    pallas_call x1, Pallas kernels, gather(): pl.pallas_call(gather_kernel, out_shape=(jax.ShapeDtypeStruct((BLOCKS, VA...  28 us
    pallas_call x1, Pallas kernels, exchange(): pl.pallas_call(exchange_kernel, out_shape=(jax.ShapeDtypeStruct((3, 2, 2,...  16.1 us
    pallas_call x1, Pallas kernels, evaluate(): pl.pallas_call(evaluate_kernel, out_shape=(shape, shape), in_specs=[vmem(...  10.7 us
    pallas_call x1, Pallas kernels, metric_rows(): pl.pallas_call(metrics_kernel, out_shape=(jax.ShapeDtypeStruct((1,) + bas...  1.38 us

profile of v2, /device:TPU:6, one launch (start us, length us, event | category | flops | bytes accessed | tf_op | source)
XLA Modules:
  0.0 58.5 jit_solution(15084618297571887622)
XLA Ops:
  0.6 0.0 copy-start
  0.6 0.8 %select_maximum_fusion.own_ref = f32[40,40]{1,0:T(8,128)S(1)} fusion(f32[3,8]{1,0:T(4,128)} %param.6, f32[8,40]{1,0:T(8,128)} %param.4, f32[24,40]{1,0:T(8,128)} %bitcast.7), kind=kLoop, calls=%fused_computation | loop fusion | flops 6400 | bytes 11616 | tf_op jit(solution)/shard_map/concatenate | solution.py:460
  1.4 0.8 %constant_dynamic-slice_fusion.strip = f32[3,2,8,256]{3,2,1,0:T(8,128)S(1)} fusion(f32[3,2,64,256]{3,2,1,0:T(8,128)} %n_ref.1, s32[]{:T(128)S(6)} %select_n.3), kind=kLoop, calls=%fused_computation.2 | loop fusion | bytes 98308 | tf_op jit(solution)/shard_map/dynamic_slice | solution.py:468
  2.2 28.0 %gather.1 = (f32[32,32,128]{2,1,0:T(8,128)S(1)}, f32[16,8,128]{2,1,0:T(8,128)S(1)}) custom-call(f32[40,40]{1,0:T(8,128)S(1)} %select_maximum_fusion.own_ref, f32[3,2,8,256]{3,2,1,0:T(8,128)S(1)} %constant_dynamic-slice_fusion.strip), custom_call_target="tpu_custom_call" | custom-call | tf_op jit(solution)/shard_map/gather/pallas_call | solution.py:142
  30.3 10.7 %evaluate.1 = (f32[768,128]{1,0:T(8,128)S(1)}, f32[768,128]{1,0:T(8,128)S(1)}) custom-call(f32[32,32,128]{2,1,0:T(8,128)S(1)} %get-tuple-element.8.g_ref, f32[3,2,8,256]{3,2,1,0:T(8,128)S(1)} %constant_dynamic-slice_fusion.strip, f32[16,8,128]{2,1,0:T(8,128)S(1)} %get-tuple-element.9.tiles), custom_call_target="tpu_custom_call" | custom-call | tf_op jit(solution)/shard_map/evaluate/pallas_call | solution.py:301
  41.0 16.1 %exchange.1 = (f32[3,2,2,64,128]{4,3,2,1,0:T(8,128)S(1)}, f32[2,3,2,64,128]{4,3,2,1,0:T(8,128)S(1)}) custom-call(f32[8,3,2,2,8,128]{5,4,3,2,1,0:T(8,128)S(1)} %bitcast.5, f32[8,3,2,2,8,128]{5,4,3,2,1,0:T(8,128)S(1)} %bitcast.6), custom_call_target="tpu_custom_call" | custom-call | tf_op jit(solution)/shard_map/exchange/pallas_call | solution.py:360
  57.1 0.0 copy-done
  57.1 1.4 %metrics.1 = (f32[1,3,2,64,256]{4,3,2,1,0:T(8,128)}, f32[1,10,2,64,256]{4,3,2,1,0:T(8,128)}) custom-call(f32[3,2,2,64,128]{4,3,2,1,0:T(8,128)S(1)} %get-tuple-element.12.own, f32[2,3,2,64,128]{4,3,2,1,0:T(8,128)S(1)} %get-tuple-element.13.halo, f32[3,2,64,256]{3,2,1,0:T(8,128)S(1)} %copy-done), custom_call_target="tpu_custom_call" | custom-call | tf_op jit(solution)/shard_map/metrics/pallas_call | solution.py:440
Async XLA Ops:
  0.6 56.5 %copy-start = (f32[3,2,64,256]{3,2,1,0:T(8,128)S(1)}, f32[3,2,64,256]{3,2,1,0:T(8,128)}, u32[]{:S(2)}) copy-start(f32[3,2,64,256]{3,2,1,0:T(8,128)} %n_ref.1) | copy-start | bytes 1179652

commit v3 on v2

--- a/solution.py
+++ b/solution.py
@@ -15,6 +15,7 @@
 VALUES = 32
 BINS = 32
 CHUNK = 128
+GROUP = 8
 PLACED = 256
 MARGIN = 1.0 + 2.0**-11
 VMEM_LIMIT = 48 * 1024 * 1024
@@ -41,7 +42,7 @@
     return arrays
 
 
-def gather_kernel(own_ref, strip, out_ref, tiles, zbuf, send, recv):
+def gather_kernel(own_ref, out_ref, zbuf, send, recv):
     inst, space = lax.axis_index("inst"), lax.axis_index("space")
     y, core = inst // CORES, inst % CORES
     x, z = space // ZS, space % ZS
@@ -81,6 +82,79 @@
         axis=0,
     )
 
+    pl.semaphore_wait(barrier, len(peers))
+
+    def start(ref, k, peer):
+        copy = pltpu.make_async_remote_copy(
+            src_ref=ref,
+            dst_ref=ref,
+            send_sem=send.at[k],
+            recv_sem=recv.at[k],
+            device_id=peer,
+            device_id_type=MESH,
+        )
+        copy.start()
+        return copy
+
+    far_first = sorted(range(ZS - 1), key=lambda k: -min(k + 1, ZS - 1 - k))
+    copies = [start(zbuf.at[z], k, z_peers[k]) for k in far_first]
+    for copy in reversed(copies):
+        copy.wait()
+    rows = jnp.concatenate([zbuf[i] for i in range(ZS)], axis=0)
+    rows = jnp.concatenate([rows, jnp.zeros((128 - 2 * ZS, 128), jnp.float32)], axis=0).T
+    block = rows[0:VALUES]
+    for a in range(1, 4):
+        block = block + pltpu.roll(rows[VALUES * a : VALUES * (a + 1)], VALUES * a, 1)
+    mine = core * (XS * YS) + y * XS + x
+    out_ref[mine] = block
+
+    def hops(k):
+        a, b = steps[k]
+        return min(a, YS - a) + min(b, XS - b)
+
+    far_first = sorted(range(len(steps)), key=lambda k: -hops(k))
+    copies = [start(out_ref.at[mine], ZS - 1 + k, plane_peers[k]) for k in far_first]
+    passed = [start(out_ref.at[mine], ZS - 1 + len(steps), other)]
+    for copy, k in reversed(list(zip(copies, far_first))):
+        copy.wait_recv()
+        a, b = steps[k]
+        origin = core * (XS * YS) + lax.rem(y + YS - a, YS) * XS + lax.rem(x + XS - b, XS)
+        passed.append(start(out_ref.at[origin], ZS + len(steps) + k, other))
+    for copy in copies:
+        copy.wait_send()
+    for copy in passed:
+        copy.wait()
+
+
+def gather(own):
+    count = ZS + 2 * XS * YS - 2
+    return pl.pallas_call(
+        gather_kernel,
+        out_shape=jax.ShapeDtypeStruct((BLOCKS, VALUES, 128), jnp.float32),
+        in_specs=[vmem()],
+        out_specs=vmem(),
+        scratch_shapes=[
+            pltpu.VMEM((ZS, 2, 128), jnp.float32),
+            pltpu.SemaphoreType.DMA((count,)),
+            pltpu.SemaphoreType.DMA((count,)),
+        ],
+        compiler_params=params(collective_id=0, has_side_effects=True),
+        cost_estimate=pl.CostEstimate(flops=10**9, bytes_accessed=2 * 10**7, transcendentals=0),
+        name="gather",
+    )(own)
+
+
+def whole_dot(a, b, precision=None):
+    return jnp.dot(a, b, precision=precision, preferred_element_type=jnp.float32)
+
+
+def evaluate_kernel(g_ref, n_ref, moved_ref, deformed_ref, kept, strip, tiles, nodes, parts, order, weights, windows, centres, found, edges, ends, arrived, passing):
+    keep = pltpu.make_async_copy(n_ref, kept, passing)
+    keep.start()
+    first = pl.multiple_of(lax.axis_index("inst") * 8, 8)
+    strip[...] = n_ref[:, :, pl.ds(first, 8), :]
+    nodes[...] = strip[...] * 0.25
+
     for half in range(2):
         lanes = slice(half * 128, half * 128 + 128)
         rows = [
@@ -93,77 +167,6 @@
         ]
         for t, tile in enumerate(swap_blocks(rows)):
             tiles[8 * half + t] = tile * 0.25
-    pl.semaphore_wait(barrier, len(peers))
-
-    def start(ref, k, peer):
-        copy = pltpu.make_async_remote_copy(
-            src_ref=ref,
-            dst_ref=ref,
-            send_sem=send.at[k],
-            recv_sem=recv.at[k],
-            device_id=peer,
-            device_id_type=MESH,
-        )
-        copy.start()
-        return copy
-
-    far_first = sorted(range(ZS - 1), key=lambda k: -min(k + 1, ZS - 1 - k))
-    copies = [start(zbuf.at[z], k, z_peers[k]) for k in far_first]
-    for copy in reversed(copies):
-        copy.wait()
-    rows = jnp.concatenate([zbuf[i] for i in range(ZS)], axis=0)
-    rows = jnp.concatenate([rows, jnp.zeros((128 - 2 * ZS, 128), jnp.float32)], axis=0).T
-    block = rows[0:VALUES]
-    for a in range(1, 4):
-        block = block + pltpu.roll(rows[VALUES * a : VALUES * (a + 1)], VALUES * a, 1)
-    mine = core * (XS * YS) + y * XS + x
-    out_ref[mine] = block
-
-    def hops(k):
-        a, b = steps[k]
-        return min(a, YS - a) + min(b, XS - b)
-
-    far_first = sorted(range(len(steps)), key=lambda k: -hops(k))
-    copies = [start(out_ref.at[mine], ZS - 1 + k, plane_peers[k]) for k in far_first]
-    passed = [start(out_ref.at[mine], ZS - 1 + len(steps), other)]
-    for copy, k in reversed(list(zip(copies, far_first))):
-        copy.wait_recv()
-        a, b = steps[k]
-        origin = core * (XS * YS) + lax.rem(y + YS - a, YS) * XS + lax.rem(x + XS - b, XS)
-        passed.append(start(out_ref.at[origin], ZS + len(steps) + k, other))
-    for copy in copies:
-        copy.wait_send()
-    for copy in passed:
-        copy.wait()
-
-
-def gather(own, strip):
-    count = ZS + 2 * XS * YS - 2
-    return pl.pallas_call(
-        gather_kernel,
-        out_shape=(
-            jax.ShapeDtypeStruct((BLOCKS, VALUES, 128), jnp.float32),
-            jax.ShapeDtypeStruct((16, 8, 128), jnp.float32),
-        ),
-        in_specs=[vmem()] * 2,
-        out_specs=(vmem(), vmem()),
-        scratch_shapes=[
-            pltpu.VMEM((ZS, 2, 128), jnp.float32),
-            pltpu.SemaphoreType.DMA((count,)),
-            pltpu.SemaphoreType.DMA((count,)),
-        ],
-        compiler_params=params(collective_id=0, has_side_effects=True),
-        name="gather",
-    )(own, strip)
-
-
-def whole_dot(a, b, precision=None):
-    return jnp.dot(a, b, precision=precision, preferred_element_type=jnp.float32)
-
-
-def evaluate_kernel(g_ref, strip, tiles, moved_ref, deformed_ref, nodes, parts, order, weights, centres, found, edges, ends, arrived):
-    nodes[...] = strip[...] * 0.25
-
     spots = [g_ref[:, 24 + c, :] * 0.25 for c in range(3)]
     near = None
     for c in range(3):
@@ -211,8 +214,13 @@
     wide_total = jnp.concatenate([total, total], axis=1)
     start = jnp.sum(jnp.where(wide_id < bin_of(k_min - MARGIN), wide_total, 0.0), axis=0, keepdims=True)
     stop = jnp.sum(jnp.where(wide_id <= bin_of(k_max + MARGIN), wide_total, 0.0), axis=0, keepdims=True)
-    edges[0:1, :] = jnp.floor(start * (1.0 / CHUNK)).astype(jnp.int32)
-    edges[1:2, :] = jnp.floor((stop + (CHUNK - 1.0)) * (1.0 / CHUNK)).astype(jnp.int32)
+    begin = jnp.floor(start * (1.0 / 32.0))
+    count = jnp.floor((jnp.maximum(stop - 32.0 * begin, 1.0) + (CHUNK - 1.0)) * (1.0 / CHUNK))
+    edges[0:1, :] = begin.astype(jnp.int32)
+    edges[1:2, :] = count.astype(jnp.int32)
+    at_tile = lax.broadcasted_iota(jnp.int32, (1, 256), 1) % 16 == 15
+    beyond = jnp.max(jnp.where(at_tile, count - 1.0, 0.0), axis=1, keepdims=True)
+    edges[3:4, :] = jnp.broadcast_to(beyond, (1, 256)).astype(jnp.int32)
     edges[2:3, :] = jnp.floor(
         (jnp.sum(wide_total, axis=0, keepdims=True) + (PLACED - 1.0)) * (1.0 / PLACED)
     ).astype(jnp.int32)
@@ -243,9 +251,9 @@
         wanted = [(slot + (s * PLACED + 128 * half)).astype(jnp.float32) for half in range(2)]
         for i in range(BLOCKS // 2):
             at = order[i * 256 : i * 256 + 256, :]
-            hit = jnp.concatenate([(at == w).astype(jnp.float32) for w in wanted], axis=1)
+            hit = jnp.concatenate([jnp.where(at == w, 1.0, 0.0) for w in wanted], axis=1)
             sums = sums + whole_dot(parts[i], hit.astype(jnp.bfloat16))
-        short = sums[0:48].astype(jnp.bfloat16)
+        short = sums[0:48]
         spot = (sums[48:56] + sums[56:64]) + sums[64:72]
         for half in range(2):
             lanes = slice(half * 128, half * 128 + 128)
@@ -258,31 +266,63 @@
 
     lax.fori_loop(0, ends[2, 0], place_chunk, 0)
 
-    for t in range(16):
-
-        def add(chunk, sums, t=t):
-            at = pl.multiple_of(chunk * CHUNK, CHUNK)
-            spot = [centres[c, pl.ds(at, CHUNK), :] for c in range(3)]
-            pieces = weights[chunk]
-            tops, rests = [], []
-            for p in range(2):
-                square = None
-                for c in range(3):
-                    gap = spot[c] - tiles[t, 2 * c + p : 2 * c + p + 1, :]
-                    square = gap * gap if square is None else square + gap * gap
-                radius = square * lax.rsqrt(jnp.maximum(square, 1e-30))
-                rest = jnp.maximum(1.0 - radius, 0.0)
-                rest = rest * rest
-                value = rest * rest * (4.0 * radius + 1.0)
-                top = value.astype(jnp.bfloat16)
-                tops.append(top)
-                rests.append((value - top.astype(jnp.float32)).astype(jnp.bfloat16))
-            full = whole_dot(pieces, jnp.concatenate(tops, axis=1))
-            extra = whole_dot(pieces[0:32], jnp.concatenate(rests, axis=1))
-            return sums + (full[0:24] + (full[24:48] + extra[0:24]))
-
-        last = 16 * t + 15
-        found[t] = lax.fori_loop(ends[0, last], ends[1, last], add, jnp.zeros((24, 256), jnp.float32))
+    behind = 2 * ends[2, 0]
+    for half in range(2):
+        weights[behind + half] = jnp.zeros((48, CHUNK), jnp.float32)
+        for c in range(3):
+            centres[c, pl.ds(pl.multiple_of((behind + half) * CHUNK, CHUNK), CHUNK), :] = jnp.zeros((CHUNK, 128), jnp.float32)
+    lane = lax.broadcasted_iota(jnp.int32, (48, CHUNK), 1)
+
+    def shift_chunk(chunk, carry):
+        here, after = weights[chunk], weights[chunk + 1]
+        windows[4 * chunk] = here.astype(jnp.bfloat16)
+        for r in range(1, 4):
+            back = CHUNK - 32 * r
+            moved = jnp.where(lane < back, pltpu.roll(here, back, 1), pltpu.roll(after, back, 1))
+            windows[4 * chunk + r] = moved.astype(jnp.bfloat16)
+        return carry
+
+    lax.fori_loop(0, behind + 1, shift_chunk, 0)
+
+    def window(t, place):
+        at = pl.multiple_of(place * 32, 32)
+        spot = [centres[c, pl.ds(at, CHUNK), :] for c in range(3)]
+        pieces = windows[place]
+        tops, rests = [], []
+        for p in range(2):
+            square = None
+            for c in range(3):
+                gap = spot[c] - tiles[t, 2 * c + p : 2 * c + p + 1, :]
+                square = gap * gap if square is None else square + gap * gap
+            radius = square * lax.rsqrt(jnp.maximum(square, 1e-30))
+            rest = jnp.maximum(1.0 - radius, 0.0)
+            rest = rest * rest
+            value = rest * rest * (4.0 * radius + 1.0)
+            top = value.astype(jnp.bfloat16)
+            tops.append(top)
+            rests.append((value - top.astype(jnp.float32)).astype(jnp.bfloat16))
+        full = whole_dot(pieces, jnp.concatenate(tops, axis=1))
+        extra = whole_dot(pieces[0:32], jnp.concatenate(rests, axis=1))
+        return full[0:24] + (full[24:48] + extra[0:24])
+
+    def first_windows(group, carry):
+        for k in range(GROUP):
+            t = group * GROUP + k
+            found[t] = window(t, ends[0, 16 * t + 15])
+        return carry
+
+    lax.fori_loop(0, 16 // GROUP, first_windows, 0)
+
+    @pl.when(ends[3, 0] > 0)
+    def _():
+        def more_windows(t, carry):
+            def one(k, carry):
+                found[t] += window(t, ends[0, 16 * t + 15] + 4 * k)
+                return carry
+
+            return lax.fori_loop(1, ends[1, 16 * t + 15], one, carry)
+
+        lax.fori_loop(0, 16, more_windows, 0)
 
     for p in range(2):
         for half in range(2):
@@ -294,30 +334,36 @@
                     into = pl.ds(c * 32 + p * 16 + half * 8 + j, 8, stride=96)
                     moved_ref[into, :] = value
                     deformed_ref[into, :] = value + strip[c, p, j : j + 1, lanes]
-
-
-def evaluate(gathered, strip, tiles):
+    keep.wait()
+
+
+def evaluate(gathered, base_nodes):
     shape = jax.ShapeDtypeStruct((INST * 96, 128), jnp.float32)
-    results = pl.pallas_call(
+    moved, deformed, kept = pl.pallas_call(
         evaluate_kernel,
-        out_shape=(shape, shape),
-        in_specs=[vmem()] * 3,
-        out_specs=(vmem(), vmem()),
+        out_shape=(shape, shape, jax.ShapeDtypeStruct(base_nodes.shape, jnp.float32)),
+        in_specs=[vmem()] * 2,
+        out_specs=(vmem(), vmem(), vmem()),
         scratch_shapes=[
+            pltpu.VMEM((3, 2, 8, 256), jnp.float32),
+            pltpu.VMEM((16, 8, 128), jnp.float32),
             pltpu.VMEM((3, 2, 8, 256), jnp.float32),
             pltpu.VMEM((BLOCKS // 2, 80, 256), jnp.bfloat16),
             pltpu.VMEM((NC, 128), jnp.float32),
-            pltpu.VMEM((NC // CHUNK, 48, CHUNK), jnp.bfloat16),
-            pltpu.VMEM((3, NC, 128), jnp.float32),
+            pltpu.VMEM((NC // CHUNK + 2, 48, CHUNK), jnp.float32),
+            pltpu.VMEM((4 * (NC // CHUNK + 1), 48, CHUNK), jnp.bfloat16),
+            pltpu.VMEM((3, NC + 2 * CHUNK, 128), jnp.float32),
             pltpu.VMEM((16, 24, 256), jnp.float32),
             pltpu.VMEM((8, 256), jnp.int32),
             pltpu.SMEM((8, 256), jnp.int32),
             pltpu.SemaphoreType.DMA,
+            pltpu.SemaphoreType.DMA,
         ],
         compiler_params=params(),
         name="evaluate",
-    )(gathered, strip, tiles)
-    return [value.reshape(INST, 3, 2, 2, 8, 128) for value in results]
+    )(gathered, base_nodes)
+    shape = (INST, 3, 2, 2, 8, 128)
+    return moved.reshape(shape), deformed.reshape(shape), kept
 
 
 def exchange_kernel(moved_ref, deformed_ref, own, halo, send, recv, local):
@@ -465,12 +511,11 @@
         ],
         axis=0,
     )
-    strip = lax.dynamic_slice_in_dim(base_nodes, lax.axis_index("inst") * 8, 8, 2)
-    gathered, tiles = gather(own, strip)
-    moved, deformed = evaluate(gathered, strip, tiles)
+    gathered = gather(own)
+    moved, deformed, nodes = evaluate(gathered, base_nodes)
     rows, width = base_nodes.shape[2], base_nodes.shape[3] // 2
     own, halo = exchange(moved, deformed, rows, width)
-    return metric_rows(own, halo, base_nodes)
+    return metric_rows(own, halo, nodes)
 
 
 def solution(mesh):

time: 58.8 us -> 56.4 us (0.959)
  the two profiles are of different devices: /device:TPU:6 before, /device:TPU:1 now
where the time goes in v3:
time: 56.4 us; the launch traced here: 56.2 us
  Pallas kernels  54.7 us (97%)
  other arithmetic  0.75 us (1%)
  between operations  0.66 us (1%)
    pallas_call x1, Pallas kernels, gather(): pl.pallas_call(gather_kernel, out_shape=jax.ShapeDtypeStruct((BLOCKS, VAL...  31 us
    pallas_call x1, Pallas kernels, exchange(): pl.pallas_call(exchange_kernel, out_shape=(jax.ShapeDtypeStruct((3, 2, 2,...  14.7 us
    pallas_call x1, Pallas kernels, evaluate(): pl.pallas_call(evaluate_kernel, out_shape=(shape, shape, jax.ShapeDtypeSt...  7.64 us
    pallas_call x1, Pallas kernels, metric_rows(): pl.pallas_call(metrics_kernel, out_shape=(jax.ShapeDtypeStruct((1,) + bas...  1.38 us

profile of v3, /device:TPU:1, one launch (start us, length us, event | category | flops | bytes accessed | tf_op | source)
XLA Modules:
  0.0 56.2 jit_solution(650208032893725644)
XLA Ops:
  0.6 0.7 %select_maximum_fusion.own_ref = f32[40,40]{1,0:T(8,128)S(1)} fusion(f32[3,8]{1,0:T(4,128)} %param.6, f32[8,40]{1,0:T(8,128)} %param.4, f32[24,40]{1,0:T(8,128)} %bitcast.7), kind=kLoop, calls=%fused_computation | loop fusion | flops 6400 | bytes 11616 | tf_op jit(solution)/shard_map/concatenate | solution.py:506
  1.4 0.0 copy-start
  1.4 31.0 %gather.1.g_ref = f32[32,32,128]{2,1,0:T(8,128)S(1)} custom-call(f32[40,40]{1,0:T(8,128)S(1)} %select_maximum_fusion.own_ref), custom_call_target="tpu_custom_call" | custom-call | flops 1000000000 | bytes 20000000 | tf_op jit(solution)/shard_map/gather/pallas_call | solution.py:131
  32.4 0.0 copy-done
  32.4 7.6 %evaluate.1 = (f32[768,128]{1,0:T(8,128)S(1)}, f32[768,128]{1,0:T(8,128)S(1)}, f32[3,2,64,256]{3,2,1,0:T(8,128)S(1)}) custom-call(f32[32,32,128]{2,1,0:T(8,128)S(1)} %gather.1.g_ref, f32[3,2,64,256]{3,2,1,0:T(8,128)S(1)} %copy-done), custom_call_target="tpu_custom_call" | custom-call | tf_op jit(solution)/shard_map/evaluate/pallas_call | solution.py:342
  40.1 14.7 %exchange.1 = (f32[3,2,2,64,128]{4,3,2,1,0:T(8,128)S(1)}, f32[2,3,2,64,128]{4,3,2,1,0:T(8,128)S(1)}) custom-call(f32[8,3,2,2,8,128]{5,4,3,2,1,0:T(8,128)S(1)} %bitcast.5, f32[8,3,2,2,8,128]{5,4,3,2,1,0:T(8,128)S(1)} %bitcast.6), custom_call_target="tpu_custom_call" | custom-call | tf_op jit(solution)/shard_map/exchange/pallas_call | solution.py:406
  54.8 1.4 %metrics.1 = (f32[1,3,2,64,256]{4,3,2,1,0:T(8,128)}, f32[1,10,2,64,256]{4,3,2,1,0:T(8,128)}) custom-call(f32[3,2,2,64,128]{4,3,2,1,0:T(8,128)S(1)} %get-tuple-element.9.own, f32[2,3,2,64,128]{4,3,2,1,0:T(8,128)S(1)} %get-tuple-element.10.halo, f32[3,2,64,256]{3,2,1,0:T(8,128)S(1)} %get-tuple-element.11.n_ref), custom_call_target="tpu_custom_call" | custom-call | tf_op jit(solution)/shard_map/metrics/pallas_call | solution.py:486
Async XLA Ops:
  1.4 31.0 %copy-start = (f32[3,2,64,256]{3,2,1,0:T(8,128)S(1)}, f32[3,2,64,256]{3,2,1,0:T(8,128)}, u32[]{:S(2)}) copy-start(f32[3,2,64,256]{3,2,1,0:T(8,128)} %n_ref.1) | copy-start | bytes 1179652

commit v4 on v3

--- a/solution.py
+++ b/solution.py
@@ -52,7 +52,13 @@
         (lax.rem(y + a, YS) * CORES + core, lax.rem(x + b, XS) * ZS + z) for a, b in steps
     ]
     other = (y * CORES + (1 - core), space)
-    peers = z_peers + plane_peers + [other]
+
+    def hops(a, b, c):
+        return min(a, ZS - a) + min(b, YS - b) + min(c, XS - c)
+
+    z_order = sorted(range(ZS - 1), key=lambda k: -hops(k + 1, 0, 0))
+    plane_order = sorted(range(len(steps)), key=lambda k: -hops(0, *steps[k]))
+    peers = [z_peers[k] for k in z_order] + [plane_peers[k] for k in plane_order] + [other]
     barrier = pltpu.get_barrier_semaphore()
     for peer in peers:
         pl.semaphore_signal(barrier, inc=1, device_id=peer, device_id_type=MESH)
@@ -96,8 +102,7 @@
         copy.start()
         return copy
 
-    far_first = sorted(range(ZS - 1), key=lambda k: -min(k + 1, ZS - 1 - k))
-    copies = [start(zbuf.at[z], k, z_peers[k]) for k in far_first]
+    copies = [start(zbuf.at[z], k, z_peers[k]) for k in z_order]
     for copy in reversed(copies):
         copy.wait()
     rows = jnp.concatenate([zbuf[i] for i in range(ZS)], axis=0)
@@ -108,14 +113,9 @@
     mine = core * (XS * YS) + y * XS + x
     out_ref[mine] = block
 
-    def hops(k):
-        a, b = steps[k]
-        return min(a, YS - a) + min(b, XS - b)
-
-    far_first = sorted(range(len(steps)), key=lambda k: -hops(k))
-    copies = [start(out_ref.at[mine], ZS - 1 + k, plane_peers[k]) for k in far_first]
+    copies = [start(out_ref.at[mine], ZS - 1 + k, plane_peers[k]) for k in plane_order]
     passed = [start(out_ref.at[mine], ZS - 1 + len(steps), other)]
-    for copy, k in reversed(list(zip(copies, far_first))):
+    for copy, k in reversed(list(zip(copies, plane_order))):
         copy.wait_recv()
         a, b = steps[k]
         origin = core * (XS * YS) + lax.rem(y + YS - a, YS) * XS + lax.rem(x + XS - b, XS)
@@ -148,25 +148,24 @@
     return jnp.dot(a, b, precision=precision, preferred_element_type=jnp.float32)
 
 
-def evaluate_kernel(g_ref, n_ref, moved_ref, deformed_ref, kept, strip, tiles, nodes, parts, order, weights, windows, centres, found, edges, ends, arrived, passing):
+def evaluate_kernel(g_ref, n_ref, moved_ref, kept, tiles, nodes, parts, order, weights, windows, centres, found, edges, ends, arrived, passing):
     keep = pltpu.make_async_copy(n_ref, kept, passing)
     keep.start()
     first = pl.multiple_of(lax.axis_index("inst") * 8, 8)
-    strip[...] = n_ref[:, :, pl.ds(first, 8), :]
-    nodes[...] = strip[...] * 0.25
+    nodes[...] = n_ref[:, :, pl.ds(first, 8), :] * 0.25
 
     for half in range(2):
         lanes = slice(half * 128, half * 128 + 128)
         rows = [
             jnp.concatenate(
-                [strip[c, p, j : j + 1, lanes] for c in range(3) for p in range(2)]
+                [nodes[c, p, j : j + 1, lanes] for c in range(3) for p in range(2)]
                 + [jnp.zeros((2, 128), jnp.float32)],
                 axis=0,
             )
             for j in range(8)
         ]
         for t, tile in enumerate(swap_blocks(rows)):
-            tiles[8 * half + t] = tile * 0.25
+            tiles[8 * half + t] = tile
     spots = [g_ref[:, 24 + c, :] * 0.25 for c in range(3)]
     near = None
     for c in range(3):
@@ -326,26 +325,22 @@
 
     for p in range(2):
         for half in range(2):
-            lanes = slice(half * 128, half * 128 + 128)
             rows = swap_blocks([found[8 * half + t, :, p * 128 : p * 128 + 128] for t in range(8)])
             for j in range(8):
                 for c in range(3):
-                    value = rows[j][c * 8 : c * 8 + 8]
                     into = pl.ds(c * 32 + p * 16 + half * 8 + j, 8, stride=96)
-                    moved_ref[into, :] = value
-                    deformed_ref[into, :] = value + strip[c, p, j : j + 1, lanes]
+                    moved_ref[into, :] = rows[j][c * 8 : c * 8 + 8]
     keep.wait()
 
 
 def evaluate(gathered, base_nodes):
     shape = jax.ShapeDtypeStruct((INST * 96, 128), jnp.float32)
-    moved, deformed, kept = pl.pallas_call(
+    moved, kept = pl.pallas_call(
         evaluate_kernel,
-        out_shape=(shape, shape, jax.ShapeDtypeStruct(base_nodes.shape, jnp.float32)),
+        out_shape=(shape, jax.ShapeDtypeStruct(base_nodes.shape, jnp.float32)),
         in_specs=[vmem()] * 2,
-        out_specs=(vmem(), vmem(), vmem()),
+        out_specs=(vmem(), vmem()),
         scratch_shapes=[
-            pltpu.VMEM((3, 2, 8, 256), jnp.float32),
             pltpu.VMEM((16, 8, 128), jnp.float32),
             pltpu.VMEM((3, 2, 8, 256), jnp.float32),
             pltpu.VMEM((BLOCKS // 2, 80, 256), jnp.bfloat16),
@@ -362,47 +357,75 @@
         compiler_params=params(),
         name="evaluate",
     )(gathered, base_nodes)
-    shape = (INST, 3, 2, 2, 8, 128)
-    return moved.reshape(shape), deformed.reshape(shape), kept
-
-
-def exchange_kernel(moved_ref, deformed_ref, own, halo, send, recv, local):
+    return moved.reshape(INST, 3, 2, 2, 8, 128), kept
+
+
+def exchange_kernel(moved_ref, n_ref, own, halo, deformed, send, recv, send_on, recv_on):
     inst, space = lax.axis_index("inst"), lax.axis_index("space")
     behind, ahead = lax.rem(space + SPACE - 1, SPACE), lax.rem(space + 1, SPACE)
+    order = (4, 3, 5, 2, 6, 1, 7)
+    peers = [(lax.rem(inst + k, INST), space) for k in order] + [(inst, behind), (inst, ahead)]
     barrier = pltpu.get_barrier_semaphore()
-    targets = [lax.rem(inst + k, INST) for k in range(INST)]
-    peers = [(t, s) for t in targets for s in (behind, ahead)] + [(t, space) for t in targets[1:]]
     for peer in peers:
         pl.semaphore_signal(barrier, inc=1, device_id=peer, device_id_type=MESH)
-    rows = pl.ds(pl.multiple_of(inst * 8, 8), 8)
-    stays = pltpu.make_async_copy(moved_ref.at[inst], own.at[:, :, :, rows, :], local)
-    stays.start()
-    pl.semaphore_wait(barrier, len(peers))
-    copies = []
-
-    def start(source, target, kind, k, device):
+
+    def start(source, target, sent, arrived, device):
         copy = pltpu.make_async_remote_copy(
             src_ref=source,
             dst_ref=target,
-            send_sem=send.at[kind, k],
-            recv_sem=recv.at[kind, k],
+            send_sem=sent,
+            recv_sem=arrived,
             device_id=device,
             device_id_type=MESH,
         )
         copy.start()
-        copies.append(copy)
-
-    for k in (4, 3, 5, 2, 6, 1, 7, 0):
-        t = targets[k]
-        start(deformed_ref.at[t, :, 0], halo.at[1, :, :, rows, :], 0, k, (t, behind))
-        start(deformed_ref.at[t, :, 1], halo.at[0, :, :, rows, :], 1, k, (t, ahead))
-        if k:
-            start(moved_ref.at[t], own.at[:, :, :, rows, :], 2, k, (t, space))
-    for copy in [stays] + copies:
+        return copy
+
+    def rows_of(strip):
+        return pl.ds(pl.multiple_of(strip * 8, 8), 8)
+
+    def add_nodes(rows):
+        for c in range(3):
+            for p in range(2):
+                nodes = n_ref[c, p, rows, :]
+                for half in range(2):
+                    lanes = slice(half * 128, half * 128 + 128)
+                    deformed[p, c, half, rows, :] = own[c, p, half, rows, :] + nodes[:, lanes]
+
+    def pass_on(k, rows):
+        return [
+            start(
+                deformed.at[side, :, :, rows, :],
+                halo.at[1 - side, :, :, rows, :],
+                send_on.at[side, k],
+                recv_on.at[side, k],
+                (inst, (behind, ahead)[side]),
+            )
+            for side in range(2)
+        ]
+
+    mine = rows_of(inst)
+    own[:, :, :, mine, :] = moved_ref[inst]
+    add_nodes(mine)
+    pl.semaphore_wait(barrier, len(peers))
+    copies = [
+        start(moved_ref.at[peer[0]], own.at[:, :, :, mine, :], send.at[k], recv.at[k], peer)
+        for k, peer in zip(order, peers)
+    ]
+    passed = pass_on(0, mine)
+    for k, copy in reversed(list(zip(order, copies))):
+        copy.wait_recv()
+        rows = rows_of(lax.rem(inst + INST - k, INST))
+        add_nodes(rows)
+        passed += pass_on(k, rows)
+    for copy in copies:
+        copy.wait_send()
+    for copy in passed:
         copy.wait()
 
 
-def exchange(moved, deformed, rows, width):
+def exchange(moved, base_nodes):
+    rows, width = base_nodes.shape[2], base_nodes.shape[3] // 2
     return pl.pallas_call(
         exchange_kernel,
         out_shape=(
@@ -412,13 +435,15 @@
         in_specs=[vmem(), vmem()],
         out_specs=(vmem(), vmem()),
         scratch_shapes=[
-            pltpu.SemaphoreType.DMA((3, INST)),
-            pltpu.SemaphoreType.DMA((3, INST)),
-            pltpu.SemaphoreType.DMA,
+            pltpu.VMEM((2, 3, 2, rows, width), jnp.float32),
+            pltpu.SemaphoreType.DMA((INST,)),
+            pltpu.SemaphoreType.DMA((INST,)),
+            pltpu.SemaphoreType.DMA((2, INST)),
+            pltpu.SemaphoreType.DMA((2, INST)),
         ],
         compiler_params=params(collective_id=1, has_side_effects=True),
         name="exchange",
-    )(moved, deformed)
+    )(moved, base_nodes)
 
 
 def shifted(value, axis):
@@ -512,9 +537,8 @@
         axis=0,
     )
     gathered = gather(own)
-    moved, deformed, nodes = evaluate(gathered, base_nodes)
-    rows, width = base_nodes.shape[2], base_nodes.shape[3] // 2
-    own, halo = exchange(moved, deformed, rows, width)
+    moved, nodes = evaluate(gathered, base_nodes)
+    own, halo = exchange(moved, nodes)
     return metric_rows(own, halo, nodes)
 
 

time: 56.4 us -> 54.9 us (0.973)
  Pallas kernels: 54.7 us -> 53.2 us
    pallas_call x1, Pallas kernels: 7.64 us -> 5.16 us  [evaluate(): pl.pallas_call(evaluate_kernel, out_shape=(shape, jax.ShapeDtypeStruct(ba...]
    pallas_call x1, Pallas kernels: 14.7 us -> 15.7 us  [exchange(): pl.pallas_call(exchange_kernel, out_shape=(jax.ShapeDtypeStruct((3, 2, 2,...]
where the time goes in v4:
time: 54.9 us; the launch traced here: 54.6 us
  Pallas kernels  53.2 us (97%)
  other arithmetic  0.75 us (1%)
  between operations  0.66 us (1%)
    pallas_call x1, Pallas kernels, gather(): pl.pallas_call(gather_kernel, out_shape=jax.ShapeDtypeStruct((BLOCKS, VAL...  31 us
    pallas_call x1, Pallas kernels, exchange(): pl.pallas_call(exchange_kernel, out_shape=(jax.ShapeDtypeStruct((3, 2, 2,...  15.7 us
    pallas_call x1, Pallas kernels, evaluate(): pl.pallas_call(evaluate_kernel, out_shape=(shape, jax.ShapeDtypeStruct(ba...  5.16 us
    pallas_call x1, Pallas kernels, metric_rows(): pl.pallas_call(metrics_kernel, out_shape=(jax.ShapeDtypeStruct((1,) + bas...  1.38 us

profile of v4, /device:TPU:1, one launch (start us, length us, event | category | flops | bytes accessed | tf_op | source)
XLA Modules:
  0.0 54.6 jit_solution(3308672395851306025)
XLA Ops:
  0.6 0.7 %select_maximum_fusion.own_ref = f32[40,40]{1,0:T(8,128)S(1)} fusion(f32[3,8]{1,0:T(4,128)} %param.6, f32[8,40]{1,0:T(8,128)} %param.4, f32[24,40]{1,0:T(8,128)} %bitcast.5), kind=kLoop, calls=%fused_computation | loop fusion | flops 6400 | bytes 11616 | tf_op jit(solution)/shard_map/concatenate | solution.py:531
  1.4 0.0 copy-start
  1.4 31.0 %gather.1.g_ref = f32[32,32,128]{2,1,0:T(8,128)S(1)} custom-call(f32[40,40]{1,0:T(8,128)S(1)} %select_maximum_fusion.own_ref), custom_call_target="tpu_custom_call" | custom-call | flops 1000000000 | bytes 20000000 | tf_op jit(solution)/shard_map/gather/pallas_call | solution.py:131
  32.4 0.0 copy-done
  32.4 5.2 %evaluate.1 = (f32[768,128]{1,0:T(8,128)S(1)}, f32[3,2,64,256]{3,2,1,0:T(8,128)S(1)}) custom-call(f32[32,32,128]{2,1,0:T(8,128)S(1)} %gather.1.g_ref, f32[3,2,64,256]{3,2,1,0:T(8,128)S(1)} %copy-done), custom_call_target="tpu_custom_call" | custom-call | tf_op jit(solution)/shard_map/evaluate/pallas_call | solution.py:338
  37.5 15.7 %exchange.1 = (f32[3,2,2,64,128]{4,3,2,1,0:T(8,128)S(1)}, f32[2,3,2,64,128]{4,3,2,1,0:T(8,128)S(1)}) custom-call(f32[8,3,2,2,8,128]{5,4,3,2,1,0:T(8,128)S(1)} %bitcast.4, f32[3,2,64,256]{3,2,1,0:T(8,128)S(1)} %get-tuple-element.7.n_ref), custom_call_target="tpu_custom_call" | custom-call | tf_op jit(solution)/shard_map/exchange/pallas_call | solution.py:429
  53.2 1.4 %metrics.1 = (f32[1,3,2,64,256]{4,3,2,1,0:T(8,128)}, f32[1,10,2,64,256]{4,3,2,1,0:T(8,128)}) custom-call(f32[3,2,2,64,128]{4,3,2,1,0:T(8,128)S(1)} %get-tuple-element.8.own, f32[2,3,2,64,128]{4,3,2,1,0:T(8,128)S(1)} %get-tuple-element.9.halo, f32[3,2,64,256]{3,2,1,0:T(8,128)S(1)} %get-tuple-element.7.n_ref), custom_call_target="tpu_custom_call" | custom-call | tf_op jit(solution)/shard_map/metrics/pallas_call | solution.py:511
Async XLA Ops:
  1.4 31.0 %copy-start = (f32[3,2,64,256]{3,2,1,0:T(8,128)S(1)}, f32[3,2,64,256]{3,2,1,0:T(8,128)}, u32[]{:S(2)}) copy-start(f32[3,2,64,256]{3,2,1,0:T(8,128)} %n_ref.1) | copy-start | bytes 1179652

commit v5 on v4

--- a/solution.py
+++ b/solution.py
@@ -219,12 +219,10 @@
     edges[1:2, :] = count.astype(jnp.int32)
     at_tile = lax.broadcasted_iota(jnp.int32, (1, 256), 1) % 16 == 15
     beyond = jnp.max(jnp.where(at_tile, count - 1.0, 0.0), axis=1, keepdims=True)
-    edges[3:4, :] = jnp.broadcast_to(beyond, (1, 256)).astype(jnp.int32)
-    edges[2:3, :] = jnp.floor(
-        (jnp.sum(wide_total, axis=0, keepdims=True) + (PLACED - 1.0)) * (1.0 / PLACED)
-    ).astype(jnp.int32)
+    edges[2:3, :] = jnp.broadcast_to(beyond, (1, 256)).astype(jnp.int32)
     copy = pltpu.make_async_copy(edges, ends, arrived)
     copy.start()
+    chunks = (jnp.sum(total[:, 0:1]).astype(jnp.int32) + (PLACED - 1)) // PLACED
 
     def split(i, carry):
         for half in range(2):
@@ -241,7 +239,6 @@
         return carry
 
     lax.fori_loop(0, BLOCKS // 2, split, 0)
-    copy.wait()
 
     slot = lax.broadcasted_iota(jnp.int32, (1, 128), 1)
 
@@ -263,25 +260,29 @@
                 centres[c, pl.ds(at, 128), :] = jnp.broadcast_to(piece[:, c : c + 1], (128, 128))
         return carry
 
-    lax.fori_loop(0, ends[2, 0], place_chunk, 0)
-
-    behind = 2 * ends[2, 0]
+    lax.fori_loop(0, chunks, place_chunk, 0)
+
+    behind = 2 * chunks
     for half in range(2):
         weights[behind + half] = jnp.zeros((48, CHUNK), jnp.float32)
         for c in range(3):
             centres[c, pl.ds(pl.multiple_of((behind + half) * CHUNK, CHUNK), CHUNK), :] = jnp.zeros((CHUNK, 128), jnp.float32)
     lane = lax.broadcasted_iota(jnp.int32, (48, CHUNK), 1)
 
-    def shift_chunk(chunk, carry):
-        here, after = weights[chunk], weights[chunk + 1]
-        windows[4 * chunk] = here.astype(jnp.bfloat16)
-        for r in range(1, 4):
-            back = CHUNK - 32 * r
-            moved = jnp.where(lane < back, pltpu.roll(here, back, 1), pltpu.roll(after, back, 1))
-            windows[4 * chunk + r] = moved.astype(jnp.bfloat16)
+    def shift_chunks(s, carry):
+        values = [weights[2 * s + k] for k in range(3)]
+        for k in range(2):
+            place = 4 * (2 * s + k)
+            windows[place] = values[k].astype(jnp.bfloat16)
+            for r in range(1, 4):
+                back = CHUNK - 32 * r
+                moved = jnp.where(lane < back, pltpu.roll(values[k], back, 1), pltpu.roll(values[k + 1], back, 1))
+                windows[place + r] = moved.astype(jnp.bfloat16)
         return carry
 
-    lax.fori_loop(0, behind + 1, shift_chunk, 0)
+    lax.fori_loop(0, chunks, shift_chunks, 0)
+    for r in range(4):
+        windows[4 * behind + r] = jnp.zeros((48, CHUNK), jnp.bfloat16)
 
     def window(t, place):
         at = pl.multiple_of(place * 32, 32)
@@ -304,6 +305,8 @@
         extra = whole_dot(pieces[0:32], jnp.concatenate(rests, axis=1))
         return full[0:24] + (full[24:48] + extra[0:24])
 
+    copy.wait()
+
     def first_windows(group, carry):
         for k in range(GROUP):
             t = group * GROUP + k
@@ -312,7 +315,7 @@
 
     lax.fori_loop(0, 16 // GROUP, first_windows, 0)
 
-    @pl.when(ends[3, 0] > 0)
+    @pl.when(ends[2, 0] > 0)
     def _():
         def more_windows(t, carry):
             def one(k, carry):
@@ -363,8 +366,13 @@
 def exchange_kernel(moved_ref, n_ref, own, halo, deformed, send, recv, send_on, recv_on):
     inst, space = lax.axis_index("inst"), lax.axis_index("space")
     behind, ahead = lax.rem(space + SPACE - 1, SPACE), lax.rem(space + 1, SPACE)
-    order = (4, 3, 5, 2, 6, 1, 7)
-    peers = [(lax.rem(inst + k, INST), space) for k in order] + [(inst, behind), (inst, ahead)]
+    y, core = inst // CORES, inst % CORES
+
+    def device(a, other):
+        return lax.rem(y + a, YS) * CORES + (1 - core if other else core)
+
+    order = [(0, 1)] + [(a, other) for a in (1, YS - 1, 2) for other in (0, 1)]
+    peers = [(device(*step), space) for step in order] + [(inst, behind), (inst, ahead)]
     barrier = pltpu.get_barrier_semaphore()
     for peer in peers:
         pl.semaphore_signal(barrier, inc=1, device_id=peer, device_id_type=MESH)
@@ -410,12 +418,12 @@
     pl.semaphore_wait(barrier, len(peers))
     copies = [
         start(moved_ref.at[peer[0]], own.at[:, :, :, mine, :], send.at[k], recv.at[k], peer)
-        for k, peer in zip(order, peers)
+        for k, peer in enumerate(peers[: len(order)])
     ]
-    passed = pass_on(0, mine)
-    for k, copy in reversed(list(zip(order, copies))):
+    passed = pass_on(len(order), mine)
+    for k, (copy, (a, other)) in enumerate(zip(copies, order)):
         copy.wait_recv()
-        rows = rows_of(lax.rem(inst + INST - k, INST))
+        rows = rows_of(device(YS - a, other))
         add_nodes(rows)
         passed += pass_on(k, rows)
     for copy in copies:
@@ -499,9 +507,13 @@
         two = cross(along_k, along_i)
         three = cross(along_i, along_j)
         last = along_i[0] * one[0] + along_i[1] * one[1] + along_i[2] * one[2]
-        for row, value in enumerate(one + two + three + [last]):
-            metrics[p, row] = value
-        leave(metrics.at[p], metrics_hbm.at[0, :, p])
+        row = 0
+        for group in (one, two, three, [last]):
+            for k, value in enumerate(group):
+                metrics[p, row + k] = value
+            rows = pl.ds(row, len(group))
+            leave(metrics.at[p, rows], metrics_hbm.at[0, rows, p])
+            row += len(group)
     for copy in copies:
         copy.wait()
 
@@ -519,7 +531,7 @@
         scratch_shapes=[
             pltpu.VMEM(base_nodes.shape, jnp.float32),
             pltpu.VMEM((2, 10) + base_nodes.shape[2:], jnp.float32),
-            pltpu.SemaphoreType.DMA((3,)),
+            pltpu.SemaphoreType.DMA((9,)),
         ],
         compiler_params=params(),
         name="metrics",

time: 54.9 us -> 54.6 us (level)
    pallas_call x1, Pallas kernels: 15.7 us -> 14.9 us  [exchange(): pl.pallas_call(exchange_kernel, out_shape=(jax.ShapeDtypeStruct((3, 2, 2,...]
where the time goes in v5:
time: 54.6 us; the launch traced here: 54.3 us
  Pallas kernels  52.9 us (97%)
  other arithmetic  0.75 us (1%)
  between operations  0.66 us (1%)
    pallas_call x1, Pallas kernels, gather(): pl.pallas_call(gather_kernel, out_shape=jax.ShapeDtypeStruct((BLOCKS, VAL...  31 us
    pallas_call x1, Pallas kernels, exchange(): pl.pallas_call(exchange_kernel, out_shape=(jax.ShapeDtypeStruct((3, 2, 2,...  14.9 us
    pallas_call x1, Pallas kernels, evaluate(): pl.pallas_call(evaluate_kernel, out_shape=(shape, jax.ShapeDtypeStruct(ba...  5.63 us
    pallas_call x1, Pallas kernels, metric_rows(): pl.pallas_call(metrics_kernel, out_shape=(jax.ShapeDtypeStruct((1,) + bas...  1.44 us

profile of v5, /device:TPU:1, one launch (start us, length us, event | category | flops | bytes accessed | tf_op | source)
XLA Modules:
  0.0 54.3 jit_solution(10348144919178785888)
XLA Ops:
  0.6 0.7 %select_maximum_fusion.own_ref = f32[40,40]{1,0:T(8,128)S(1)} fusion(f32[3,8]{1,0:T(4,128)} %param.6, f32[8,40]{1,0:T(8,128)} %param.4, f32[24,40]{1,0:T(8,128)} %bitcast.5), kind=kLoop, calls=%fused_computation | loop fusion | flops 6400 | bytes 11616 | tf_op jit(solution)/shard_map/concatenate | solution.py:543
  1.4 0.0 copy-start
  1.4 31.0 %gather.1.g_ref = f32[32,32,128]{2,1,0:T(8,128)S(1)} custom-call(f32[40,40]{1,0:T(8,128)S(1)} %select_maximum_fusion.own_ref), custom_call_target="tpu_custom_call" | custom-call | flops 1000000000 | bytes 20000000 | tf_op jit(solution)/shard_map/gather/pallas_call | solution.py:131
  32.4 0.0 copy-done
  32.4 5.6 %evaluate.1 = (f32[768,128]{1,0:T(8,128)S(1)}, f32[3,2,64,256]{3,2,1,0:T(8,128)S(1)}) custom-call(f32[32,32,128]{2,1,0:T(8,128)S(1)} %gather.1.g_ref, f32[3,2,64,256]{3,2,1,0:T(8,128)S(1)} %copy-done), custom_call_target="tpu_custom_call" | custom-call | tf_op jit(solution)/shard_map/evaluate/pallas_call | solution.py:341
  38.0 14.9 %exchange.1 = (f32[3,2,2,64,128]{4,3,2,1,0:T(8,128)S(1)}, f32[2,3,2,64,128]{4,3,2,1,0:T(8,128)S(1)}) custom-call(f32[8,3,2,2,8,128]{5,4,3,2,1,0:T(8,128)S(1)} %bitcast.4, f32[3,2,64,256]{3,2,1,0:T(8,128)S(1)} %get-tuple-element.7.n_ref), custom_call_target="tpu_custom_call" | custom-call | tf_op jit(solution)/shard_map/exchange/pallas_call | solution.py:437
  52.9 1.4 %metrics.1 = (f32[1,3,2,64,256]{4,3,2,1,0:T(8,128)}, f32[1,10,2,64,256]{4,3,2,1,0:T(8,128)}) custom-call(f32[3,2,2,64,128]{4,3,2,1,0:T(8,128)S(1)} %get-tuple-element.8.own, f32[2,3,2,64,128]{4,3,2,1,0:T(8,128)S(1)} %get-tuple-element.9.halo, f32[3,2,64,256]{3,2,1,0:T(8,128)S(1)} %get-tuple-element.7.n_ref), custom_call_target="tpu_custom_call" | custom-call | tf_op jit(solution)/shard_map/metrics/pallas_call | solution.py:523
Async XLA Ops:
  1.4 31.0 %copy-start = (f32[3,2,64,256]{3,2,1,0:T(8,128)S(1)}, f32[3,2,64,256]{3,2,1,0:T(8,128)}, u32[]{:S(2)}) copy-start(f32[3,2,64,256]{3,2,1,0:T(8,128)} %n_ref.1) | copy-start | bytes 1179652
